TPU v7x, 32 devices: a whole 2x2x4 slice. The times are simulated.
32 devices in a mesh: plane: 4 (over y, x), tile: 8 (over z, core).
Axes of the slice: x: 2, y: 2, z: 4, core: 2. Of those that a mesh axis runs over, the one named last changes fastest.
Arguments:
- density: float32 [12, 64, 2048], P('plane', 'tile'), may hold values from -6 to 6
- plane_slot: int32 [12], replicated, may hold values from 0 to 23, as said below
- paint_weight: float32 [32, 9], replicated, may hold values from -2 to 2
- paint_bias: float32 [32], replicated, may hold values from -0.5 to 0.5
- mix_weight: float32 [32], replicated, may hold values from -1 to 1
- short_kernel: float32 [5, 5], replicated, may hold values from -1 to 1
Outputs:
- distortion: float32 [4, 12, 64, 2048], P(None, 'plane', 'tile')
Inputs may be any that keep to these rules, and one draw needn't show every extreme that they name: `plane_slot`: strictly increasing along the planes; the first is 0 and the last is 23.
All inputs are finite; a program needn't handle non-finite values.
Results may differ from a plain program's by a relative error of at most 0.00026.
Values sent between devices are 32-bit elements; how exact they have to be, the bound alone decides.
A program may use at most 64 MiB of HBM per device.

v0:
```python
import math

import jax
import jax.numpy as jnp
from jax import lax
from jax.sharding import PartitionSpec as P

highest = lax.Precision.HIGHEST
lens_gain = 0.25


def extended_2(block, sides, width):
    for axis, dim in sides:
        count = lax.axis_size(axis)
        forward = [(i, i + 1) for i in range(count - 1)]
        backward = [(target, source) for source, target in forward]
        low = lax.ppermute(
            lax.slice_in_dim(block, block.shape[dim] - width, None, axis=dim), axis, forward
        )
        high = lax.ppermute(lax.slice_in_dim(block, 0, width, axis=dim), axis, backward)
        block = jnp.concatenate([low, block, high], axis=dim)
    return block


def from_behind(value, axis, by):
    devices = lax.axis_size(axis)
    pairs = [(i, i + by) for i in range(devices) if 0 <= i + by < devices]
    return lax.ppermute(value, axis, pairs)


def paint_rows(extended, paint_weight, paint_bias, mix_weight):
    row_count = extended.shape[-2] - 4
    col_count = extended.shape[-1]
    padded = jnp.pad(extended, [(0, 0)] * (extended.ndim - 1) + [(2, 2)])
    stacked = jnp.stack(
        [
            padded[
                ...,
                2 + 2 * row_step : 2 + 2 * row_step + row_count,
                2 + 2 * col_step : 2 + 2 * col_step + col_count,
            ]
            for row_step in (-1, 0, 1)
            for col_step in (-1, 0, 1)
        ],
        axis=0,
    )
    before = jnp.einsum("ct,t...->c...", paint_weight, stacked, precision=highest)
    hidden = jnp.tanh(before + paint_bias.reshape((-1,) + (1,) * (before.ndim - 1)))
    return jnp.einsum("c,c...->...", mix_weight, hidden, precision=highest)


def short_rows(extended, short_kernel):
    row_count = extended.shape[-2] - 4
    col_count = extended.shape[-1]
    padded = jnp.pad(extended, [(0, 0)] * (extended.ndim - 1) + [(2, 2)])
    running = jnp.zeros(extended.shape[:-2] + (row_count, col_count), jnp.float32)
    for row_tap in range(5):
        for col_tap in range(5):
            running = (
                running
                + short_kernel[row_tap, col_tap]
                * padded[..., row_tap : row_tap + row_count, col_tap : col_tap + col_count]
            )
    return running


def hessian_rows(extended):
    padded = jnp.pad(extended, [(0, 0)] * (extended.ndim - 1) + [(1, 1)])
    center = padded[..., 1:-1, 1:-1]
    second_rows = padded[..., 2:, 1:-1] - 2.0 * center + padded[..., :-2, 1:-1]
    second_cols = padded[..., 1:-1, 2:] - 2.0 * center + padded[..., 1:-1, :-2]
    mixed_part = (
        padded[..., 2:, 2:] - padded[..., 2:, :-2] - padded[..., :-2, 2:] + padded[..., :-2, :-2]
    ) * 0.25
    return jnp.stack([second_rows, second_cols, mixed_part], axis=0)


def lens_step(lens_state, shear_field, mixing, bending):
    previous = lens_state[0:2]
    current = lens_state[2:4]
    bent_first = shear_field[0] * current[0] + shear_field[2] * current[1]
    bent_second = shear_field[2] * current[0] + shear_field[1] * current[1]
    bent_rows = jnp.stack([bent_first, bent_second], axis=0)
    advanced = (1.0 - mixing) * previous + mixing * current - bending * bent_rows
    return jnp.concatenate([current, advanced], axis=0)


def distances(plane_slot, slot_total):
    distance = (plane_slot.astype(jnp.float32) + 1.0) / slot_total
    before = jnp.concatenate([jnp.zeros((1,), jnp.float32), distance[:-1]])
    after = jnp.concatenate(
        [distance[1:], jnp.full((1,), (slot_total + 1.0) / slot_total, jnp.float32)]
    )
    mixing = before * (after - distance) / (distance * (after - before))
    bending = lens_gain * (after - distance) / after
    return (mixing, bending)


def coarse_kernel(row_global, col_global, scale):
    gap = row_global.astype(jnp.float32)[:, None] - col_global.astype(jnp.float32)[None, :]
    return jnp.exp(-jnp.abs(gap) / scale)


def start_for(row_count, col_count):
    pattern = jnp.array([[1.0, 0.0], [0.0, 1.0], [1.0, 0.0], [0.0, 1.0]], jnp.float32)
    return jnp.broadcast_to(pattern[:, :, None, None], (4, 2, row_count, col_count))


def body(density, plane_slot, paint_weight, paint_bias, mix_weight, short_kernel):
    plane_count, row_count, col_count = density.shape
    tile_count = lax.axis_size("tile")
    tile_index = lax.axis_index("tile")
    plane_index = lax.axis_index("plane")
    total_rows = row_count * tile_count
    coarse_here = row_count // 4
    coarse_cols = col_count // 4
    row_scale = total_rows / 16.0
    col_scale = col_count / 16.0
    long_gain = 1.0 / math.sqrt(row_scale * col_scale)
    col_kernel = coarse_kernel(
        jnp.arange(coarse_cols, dtype=jnp.int32),
        jnp.arange(coarse_cols, dtype=jnp.int32),
        col_scale,
    )
    mixing_all, bending_all = distances(plane_slot, 2 * plane_slot.shape[0])
    mixing_here = lax.dynamic_slice_in_dim(mixing_all, plane_index * plane_count, plane_count)
    bending_here = lax.dynamic_slice_in_dim(bending_all, plane_index * plane_count, plane_count)
    extended = extended_2(density, (("tile", 1),), 2)
    convergence = paint_rows(extended, paint_weight, paint_bias, mix_weight)
    convergence_wide = extended_2(convergence, (("tile", 1),), 2)
    short_part = short_rows(convergence_wide, short_kernel)
    row_global = tile_index * coarse_here + 0 + jnp.arange(coarse_here, dtype=jnp.int32)
    coarse = convergence.reshape(plane_count, coarse_here, 4, coarse_cols, 4).mean(axis=(2, 4))
    received = lax.all_gather(coarse, "tile", axis=1, tiled=True)
    span_cols = received.shape[1]
    kernel_block = coarse_kernel(row_global, jnp.arange(span_cols, dtype=jnp.int32), row_scale)
    summed = jnp.einsum("ik,pkx->pix", kernel_block, received, precision=highest)
    potential = short_part + jnp.repeat(
        jnp.repeat(
            long_gain * jnp.einsum("pix,xy->piy", summed, col_kernel, precision=highest), 4, axis=1
        ),
        4,
        axis=2,
    )
    potential_wide = extended_2(potential, (("tile", 1),), 1)
    shear_field = hessian_rows(potential_wide)

    def run_planes(lens_state):
        results = []
        for plane_pos in range(plane_count):
            lens_state = lens_step(
                lens_state,
                shear_field[:, plane_pos],
                mixing_here[plane_pos],
                bending_here[plane_pos],
            )
            results.append(lens_state[2:4].reshape(4, row_count, col_count))
        return (lens_state, jnp.stack(results, axis=1))

    start_state = start_for(row_count, col_count)

    def relay_turn(iteration, state_in):
        state_out, unused_results = run_planes(state_in)
        incoming = from_behind(state_out, "plane", 1)
        return jnp.where(plane_index == 0, start_state, incoming)

    state_in = lax.fori_loop(0, lax.axis_size("plane") - 1, relay_turn, start_state)
    unused_state, results = run_planes(state_in)
    return results


def solution(mesh):
    placed = (P("plane", "tile", None), P(), P(), P(), P(), P())
    return jax.shard_map(
        body, mesh=mesh, in_specs=placed, out_specs=P(None, "plane", "tile", None), check_vma=False
    )
```

profile of v0, /device:TPU:12, one launch (start us, length us, event | category | flops | bytes accessed | tf_op | source)
XLA Modules:
  0.0 186.6 jit_solution(18332777725113661293)
XLA Ops:
  1.1 1.9 %collective-permute-start.1 = (f32[3,2,2048]{2,1,0:T(2,128)S(1)}, f32[3,2,2048]{2,1,0:T(2,128)S(1)}, u32[]{:S(2)}, u32[]{:S(2)}) collective-permute-start(f32[3,2,2048]{2,1,0:T(2,128)S(1)} %get-tuple-element.225), channel_id=1, source_target_pairs={{0,1},{1,2},{2,3},{3,4},{4,5},{5,6},{6,7},{8,9},{9,10},{10,11},{11... | collective-permute-start | bytes 147464 | tf_op jit(solution)/shard_map/ppermute | solution.py:17
  3.0 3.6 %collective-permute-start.2 = (f32[3,2,2048]{2,1,0:T(2,128)S(1)}, f32[3,2,2048]{2,1,0:T(2,128)S(1)}, u32[]{:S(2)}, u32[]{:S(2)}) collective-permute-start(f32[3,2,2048]{2,1,0:T(2,128)S(1)} %get-tuple-element.226), channel_id=1, source_target_pairs={{1,0},{2,1},{3,2},{4,3},{5,4},{6,5},{7,6},{9,8},{10,9},{11,10},{12... | collective-permute-start | bytes 147464 | tf_op jit(solution)/shard_map/ppermute | solution.py:20
  7.8 2.1 %fusion.81 = (f32[1,1]{1,0:T(1,128)}, f32[1,1]{1,0:T(1,128)}, f32[1,1]{1,0:T(1,128)}, f32[1,1]{1,0:T(1,128)}, f32[1,1]{1,0:T(1,128)}, /*index=5*/f32[1,1]{1,0:T(...) fusion(f32[5,5]{1,0:T(8,128)} %param.14), kind=kLoop, calls=%fused_computation.183 | loop fusion | bytes 152 | tf_op jit(solution)/shard_map/slice | solution.py:61
  9.9 1.6 fusion.82
  24.1 6.6 %stack.90 = f32[9,3,8,2048]{3,0,2,1:T(8,128)S(1)} concatenate(f32[1,3,8,2048]{3,0,2,1:T(1,128)S(1)} %copy.215, f32[1,3,8,2048]{3,0,2,1:T(1,128)} %stack.82, f32[1,3,8,2048]{3,0,2,1:T(1,128)} %copy.216, f32[1,3,8,2048]{3,0,2,1:T(1,128)} %copy.217, f32[1,3,8,2048]{3,0,2,1:T(1,128)S(1)} %stack.85, f32[1,3,8,2048]{3,0,2,1:T(1,128)} %copy.218, f32[1,3,8,2048]{3,0,2,1:T(1,128)} %copy.219, ...), dimensions={0} | concatenate | bytes 3538944 | tf_op jit(solution)/shard_map/stack | solution.py:35
  30.8 7.6 %fusion.61 = f32[3,8,2048,32]{2,3,1,0:T(8,128)S(1)} fusion(f32[9,3,8,2048]{3,0,2,1:T(8,128)S(1)} %stack.90, f32[32,9]{0,1:T(8,128)S(1)} %copy-done), kind=kOutput, calls=%fused_computation.154 | convolution fusion | flops 169869312 | bytes 8062080 | tf_op jit(solution)/shard_map/ct,t...->c.../dot_general | solution.py:47
  38.4 3.8 %fusion.3 = f32[1,3,8,2048]{3,0,2,1:T(1,128)S(1)} fusion(f32[3,8,2048,32]{2,3,1,0:T(8,128)S(1)} %fusion.61, f32[32]{0:T(128)S(1)} %copy-done.5, f32[32]{0:T(128)S(1)} %copy-done.6), kind=kOutput, calls=%fused_computation.23 | convolution fusion | flops 20447232 | bytes 6488320 | tf_op jit(solution)/shard_map/c,c...->.../dot_general | solution.py:49
  43.0 7.9 %reshape.65 = f32[3,2,4,512,4]{4,3,2,1,0:T(8,128)} reshape(f32[3,8,2048]{2,1,0:T(8,128)S(1)} %bitcast.135) | data formatting | bytes 393216 | tf_op jit(solution)/shard_map/reshape | solution.py:133
  50.9 1.9 %collective-permute-start.3 = (f32[3,2,2048]{2,1,0:T(2,128)}, f32[3,2,2048]{2,1,0:T(2,128)}, u32[]{:S(2)}, u32[]{:S(2)}) collective-permute-start(f32[3,2,2048]{2,1,0:T(2,128)} %get-tuple-element.221), channel_id=1, source_target_pairs={{0,1},{1,2},{2,3},{3,4},{4,5},{5,6},{6,7},{8,9},{9,10},{10,11},{11... | collective-permute-start | bytes 147464 | tf_op jit(solution)/shard_map/ppermute | solution.py:17
  52.8 3.6 %collective-permute-start.4 = (f32[3,2,2048]{2,1,0:T(2,128)}, f32[3,2,2048]{2,1,0:T(2,128)}, u32[]{:S(2)}, u32[]{:S(2)}) collective-permute-start(f32[3,2,2048]{2,1,0:T(2,128)} %get-tuple-element.222), channel_id=1, source_target_pairs={{1,0},{2,1},{3,2},{4,3},{5,4},{6,5},{7,6},{9,8},{10,9},{11,10},{12... | collective-permute-start | bytes 147464 | tf_op jit(solution)/shard_map/ppermute | solution.py:20
  56.4 3.3 %reduce_sum.9 = f32[3,2,512]{2,1,0:T(2,128)S(1)} reduce(f32[3,2,4,512,4]{4,3,2,1,0:T(8,128)} %reshape.65, f32[]{:T(128)} %constant.53.clone.1), dimensions={2,4}, to_apply=%region_0.1 | reduce | flops 46080 | bytes 208900 | tf_op jit(solution)/shard_map/reduce_sum | solution.py:133
  59.8 14.4 %all_gather.3 = f32[3,16,512]{2,0,1:T(4,128)S(1)} all-gather(f32[3,2,512]{2,0,1:T(4,128)S(1)} %copy.220), channel_id=1, replica_groups=mesh['plane'=4,'tile'=8] {'tile'}, dimensions={1}, use_global_device_ids=true | all-gather | bytes 110592 | tf_op jit(solution)/shard_map/all_gather | solution.py:134
  76.5 1.7 broadcast_in_dim.8
  80.4 17.4 %fusion.32 = f32[3,8,2048]{2,1,0:T(8,128)S(1)} fusion(f32[3,8,2048]{2,1,0:T(8,128)S(1)} %copy.225, f32[3,8,2048]{2,1,0:T(8,128)S(1)} %bitcast.137, f32[3,2,2048]{2,1,0:T(2,128)} %collective-permute-done.4, f32[3,2,2048]{2,1,0:T(2,128)} %collective-permute-done.3, f32[3,12,2052]{2,1,0:T(8,128)S(1)} %select_maximum_fusion.2, f32[]{:T(128)} %bitcast.37, ...), kind=kLoop, calls=%fused_computation.73 | loop fusion | flops 2654208 | bytes 4620388 | tf_op jit(solution)/shard_map/add | solution.py:138
  97.9 2.4 %collective-permute-start.5 = (f32[3,1,2048]{2,1,0:T(1,128)S(1)}, f32[3,1,2048]{2,1,0:T(1,128)S(1)}, u32[]{:S(2)}, u32[]{:S(2)}) collective-permute-start(f32[3,1,2048]{2,1,0:T(1,128)S(1)} %get-tuple-element.220), channel_id=1, source_target_pairs={{1,0},{2,1},{3,2},{4,3},{5,4},{6,5},{7,6},{9,8},{10,9},{11,10},{12... | collective-permute-start | bytes 73736 | tf_op jit(solution)/shard_map/ppermute | solution.py:20
  100.3 2.0 %collective-permute-start.6 = (f32[3,1,2048]{2,1,0:T(1,128)S(1)}, f32[3,1,2048]{2,1,0:T(1,128)S(1)}, u32[]{:S(2)}, u32[]{:S(2)}) collective-permute-start(f32[3,1,2048]{2,1,0:T(1,128)S(1)} %get-tuple-element.219), channel_id=1, source_target_pairs={{0,1},{1,2},{2,3},{3,4},{4,5},{5,6},{6,7},{8,9},{9,10},{10,11},{11... | collective-permute-start | bytes 73736 | tf_op jit(solution)/shard_map/ppermute | solution.py:17
  106.2 72.7 %while.13 = (s32[]{:T(128)}, f32[4,2,8,2048]{3,2,1,0:T(8,128)S(1)}, pred[]{:T(512)}, f32[]{:T(128)}, f32[3]{0:T(128)S(1)}, /*index=5*/f32[]{:T(128)}, f32[3]{0:T...) while((s32[]{:T(128)}, f32[4,2,8,2048]{3,2,1,0:T(8,128)S(1)}, ...), condition=%wide.region_2.3_spmd.clone, body=%wide.region_1.2_spmd.sunk.clone.sunk | while | flops 2818050 | bytes 11469090 | solution.py:167
  108.3 2.6 %fusion.93 = f32[2,2,8,2048]{3,2,1,0:T(8,128)S(1)} fusion(f32[1,2,8,2048]{3,2,1,0:T(8,128)S(1)} %get-tuple-element.351, f32[1,2,8,2048]{3,2,1,0:T(8,128)S(1)} %get-tuple-element.352, f32[4,2,8,2048]{3,2,1,0:T(8,128)S(1)} %get-tuple-element.374, f32[]{:T(128)} %bitcast.128, f32[]{:T(128)} %bitcast.129, f32[]{:T(128)} %get-tuple-element.387, ...), kind=kLoop, calls=%fused_computation.4.clone.1 | loop fusion | flops 786432 | bytes 1310744 | tf_op jit(solution)/shard_map/while/body/eval_jaxpr/sub | solution.py:84
  110.9 2.7 %fusion.94 = f32[2,2,8,2048]{3,2,1,0:T(8,128)S(1)} fusion(f32[1,2,8,2048]{3,2,1,0:T(8,128)S(1)} %get-tuple-element.358, f32[1,2,8,2048]{3,2,1,0:T(8,128)S(1)} %get-tuple-element.359, f32[2,2,8,2048]{3,2,1,0:T(8,128)S(1)} %fusion.93, f32[]{:T(128)} %bitcast.130, f32[]{:T(128)} %bitcast.131, f32[]{:T(128)} %get-tuple-element.392, ...), kind=kLoop, calls=%fused_computation.6.clone.1 | loop fusion | flops 786432 | bytes 1572888 | tf_op jit(solution)/shard_map/while/body/eval_jaxpr/sub | solution.py:84
  113.7 3.4 %collective-permute-start = (f32[4,2,8,2048]{3,2,1,0:T(8,128)S(1)}, f32[4,2,8,2048]{3,2,1,0:T(8,128)S(1)}, u32[]{:S(2)}, u32[]{:S(2)}) collective-permute-start(f32[4,2,8,2048]{3,2,1,0:T(8,128)S(1)} %pad_maximum_fusion.12), channel_id=1, source_target_pairs={{0,8},{8,16},{16,24},{1,9},{9,17},{17,25},{2,10},{10,18},{18,26},{... | collective-permute-start | bytes 1572872 | tf_op jit(solution)/shard_map/while/body/eval_jaxpr/ppermute | solution.py:28
  117.1 14.1 %collective-permute-done = f32[4,2,8,2048]{3,2,1,0:T(8,128)S(1)} collective-permute-done((f32[4,2,8,2048]{3,2,1,0:T(8,128)S(1)}, f32[4,2,8,2048]{3,2,1,0:T(8,128)S(1)}, u32[]{:S(2)}, u32[]{:S(2)}) %collective-permute-start) | collective-permute-done | bytes 524320 | tf_op jit(solution)/shard_map/while/body/eval_jaxpr/ppermute | solution.py:28
  133.4 2.6 %fusion.93 = f32[2,2,8,2048]{3,2,1,0:T(8,128)S(1)} fusion(f32[1,2,8,2048]{3,2,1,0:T(8,128)S(1)} %get-tuple-element.351, f32[1,2,8,2048]{3,2,1,0:T(8,128)S(1)} %get-tuple-element.352, f32[4,2,8,2048]{3,2,1,0:T(8,128)S(1)} %get-tuple-element.374, f32[]{:T(128)} %bitcast.128, f32[]{:T(128)} %bitcast.129, f32[]{:T(128)} %get-tuple-element.387, ...), kind=kLoop, calls=%fused_computation.4.clone.1 | loop fusion | flops 786432 | bytes 1310744 | tf_op jit(solution)/shard_map/while/body/eval_jaxpr/sub | solution.py:84
  136.0 2.7 %fusion.94 = f32[2,2,8,2048]{3,2,1,0:T(8,128)S(1)} fusion(f32[1,2,8,2048]{3,2,1,0:T(8,128)S(1)} %get-tuple-element.358, f32[1,2,8,2048]{3,2,1,0:T(8,128)S(1)} %get-tuple-element.359, f32[2,2,8,2048]{3,2,1,0:T(8,128)S(1)} %fusion.93, f32[]{:T(128)} %bitcast.130, f32[]{:T(128)} %bitcast.131, f32[]{:T(128)} %get-tuple-element.392, ...), kind=kLoop, calls=%fused_computation.6.clone.1 | loop fusion | flops 786432 | bytes 1572888 | tf_op jit(solution)/shard_map/while/body/eval_jaxpr/sub | solution.py:84
  138.7 2.5 %collective-permute-start = (f32[4,2,8,2048]{3,2,1,0:T(8,128)S(1)}, f32[4,2,8,2048]{3,2,1,0:T(8,128)S(1)}, u32[]{:S(2)}, u32[]{:S(2)}) collective-permute-start(f32[4,2,8,2048]{3,2,1,0:T(8,128)S(1)} %pad_maximum_fusion.12), channel_id=1, source_target_pairs={{0,8},{8,16},{16,24},{1,9},{9,17},{17,25},{2,10},{10,18},{18,26},{... | collective-permute-start | bytes 1572872 | tf_op jit(solution)/shard_map/while/body/eval_jaxpr/ppermute | solution.py:28
  141.2 14.1 %collective-permute-done = f32[4,2,8,2048]{3,2,1,0:T(8,128)S(1)} collective-permute-done((f32[4,2,8,2048]{3,2,1,0:T(8,128)S(1)}, f32[4,2,8,2048]{3,2,1,0:T(8,128)S(1)}, u32[]{:S(2)}, u32[]{:S(2)}) %collective-permute-start) | collective-permute-done | bytes 524320 | tf_op jit(solution)/shard_map/while/body/eval_jaxpr/ppermute | solution.py:28
  157.6 2.6 %fusion.93 = f32[2,2,8,2048]{3,2,1,0:T(8,128)S(1)} fusion(f32[1,2,8,2048]{3,2,1,0:T(8,128)S(1)} %get-tuple-element.351, f32[1,2,8,2048]{3,2,1,0:T(8,128)S(1)} %get-tuple-element.352, f32[4,2,8,2048]{3,2,1,0:T(8,128)S(1)} %get-tuple-element.374, f32[]{:T(128)} %bitcast.128, f32[]{:T(128)} %bitcast.129, f32[]{:T(128)} %get-tuple-element.387, ...), kind=kLoop, calls=%fused_computation.4.clone.1 | loop fusion | flops 786432 | bytes 1310744 | tf_op jit(solution)/shard_map/while/body/eval_jaxpr/sub | solution.py:84
  160.2 2.7 %fusion.94 = f32[2,2,8,2048]{3,2,1,0:T(8,128)S(1)} fusion(f32[1,2,8,2048]{3,2,1,0:T(8,128)S(1)} %get-tuple-element.358, f32[1,2,8,2048]{3,2,1,0:T(8,128)S(1)} %get-tuple-element.359, f32[2,2,8,2048]{3,2,1,0:T(8,128)S(1)} %fusion.93, f32[]{:T(128)} %bitcast.130, f32[]{:T(128)} %bitcast.131, f32[]{:T(128)} %get-tuple-element.392, ...), kind=kLoop, calls=%fused_computation.6.clone.1 | loop fusion | flops 786432 | bytes 1572888 | tf_op jit(solution)/shard_map/while/body/eval_jaxpr/sub | solution.py:84
  163.0 1.9 %collective-permute-start = (f32[4,2,8,2048]{3,2,1,0:T(8,128)S(1)}, f32[4,2,8,2048]{3,2,1,0:T(8,128)S(1)}, u32[]{:S(2)}, u32[]{:S(2)}) collective-permute-start(f32[4,2,8,2048]{3,2,1,0:T(8,128)S(1)} %pad_maximum_fusion.12), channel_id=1, source_target_pairs={{0,8},{8,16},{16,24},{1,9},{9,17},{17,25},{2,10},{10,18},{18,26},{... | collective-permute-start | bytes 1572872 | tf_op jit(solution)/shard_map/while/body/eval_jaxpr/ppermute | solution.py:28
  164.9 13.9 %collective-permute-done = f32[4,2,8,2048]{3,2,1,0:T(8,128)S(1)} collective-permute-done((f32[4,2,8,2048]{3,2,1,0:T(8,128)S(1)}, f32[4,2,8,2048]{3,2,1,0:T(8,128)S(1)}, u32[]{:S(2)}, u32[]{:S(2)}) %collective-permute-start) | collective-permute-done | bytes 524320 | tf_op jit(solution)/shard_map/while/body/eval_jaxpr/ppermute | solution.py:28
  178.9 1.3 fusion.19
  180.3 2.5 %fusion.20 = f32[2,2,8,2048]{3,2,1,0:T(8,128)S(1)} fusion(f32[1,2,8,2048]{3,2,1,0:T(8,128)S(1)} %get-tuple-element.208, f32[1,2,8,2048]{3,2,1,0:T(8,128)S(1)} %get-tuple-element.207, f32[4,2,8,2048]{3,2,1,0:T(8,128)S(1)} %get-tuple-element.104, f32[]{:T(128)} %bitcast.51, f32[]{:T(128)} %bitcast.1, f32[]{:T(128)} %sub.90, ...), kind=kLoop, calls=%fused_computation.60 | loop fusion | flops 786432 | bytes 1310744 | tf_op jit(solution)/shard_map/sub | solution.py:84
  182.9 2.7 %fusion.21 = f32[2,2,8,2048]{3,2,1,0:T(8,128)S(1)} fusion(f32[1,2,8,2048]{3,2,1,0:T(8,128)S(1)} %get-tuple-element.206, f32[1,2,8,2048]{3,2,1,0:T(8,128)S(1)} %get-tuple-element.205, f32[2,2,8,2048]{3,2,1,0:T(8,128)S(1)} %fusion.20, f32[]{:T(128)} %bitcast.56, f32[]{:T(128)} %bitcast.45, f32[]{:T(128)} %sub.101, ...), kind=kLoop, calls=%fused_computation.62 | loop fusion | flops 786432 | bytes 1572888 | tf_op jit(solution)/shard_map/sub | solution.py:84
  (90 shorter events, 30.1 us)
Async XLA Ops:
  0.0 30.7 %copy-start = (f32[32,9]{0,1:T(8,128)S(1)}, f32[32,9]{0,1:T(8,128)}, u32[]{:S(2)}) copy-start(f32[32,9]{0,1:T(8,128)} %param.11) | copy-start | bytes 3460
  1.1 14.3 %collective-permute-start.1 = (f32[3,2,2048]{2,1,0:T(2,128)S(1)}, f32[3,2,2048]{2,1,0:T(2,128)S(1)}, u32[]{:S(2)}, u32[]{:S(2)}) collective-permute-start(f32[3,2,2048]{2,1,0:T(2,128)S(1)} %get-tuple-element.225), channel_id=1, source_target_pairs={{0,1},{1,2},{2,3},{3,4},{4,5},{5,6},{6,7},{8,9},{9,10},{10,11},{11... | collective-permute-start | bytes 147464 | tf_op jit(solution)/shard_map/ppermute | solution.py:17
  3.0 12.4 %collective-permute-start.2 = (f32[3,2,2048]{2,1,0:T(2,128)S(1)}, f32[3,2,2048]{2,1,0:T(2,128)S(1)}, u32[]{:S(2)}, u32[]{:S(2)}) collective-permute-start(f32[3,2,2048]{2,1,0:T(2,128)S(1)} %get-tuple-element.226), channel_id=1, source_target_pairs={{1,0},{2,1},{3,2},{4,3},{5,4},{6,5},{7,6},{9,8},{10,9},{11,10},{12... | collective-permute-start | bytes 147464 | tf_op jit(solution)/shard_map/ppermute | solution.py:20
  30.7 7.6 %copy-start.5 = (f32[32]{0:T(128)S(1)}, f32[32]{0:T(128)}, u32[]{:S(2)}) copy-start(f32[32]{0:T(128)} %param.12) | copy-start | bytes 388
  30.8 7.6 %copy-start.6 = (f32[32]{0:T(128)S(1)}, f32[32]{0:T(128)}, u32[]{:S(2)}) copy-start(f32[32]{0:T(128)} %param.13) | copy-start | bytes 388
  43.0 31.2 %copy-start.3 = (f32[16]{0:T(128)S(1)}, f32[16]{0:T(128)}, u32[]{:S(2)}) copy-start(f32[16]{0:T(128)} %iota_convert_fusion.1) | copy-start | bytes 196
  43.0 31.2 %copy-start.4 = (f32[2]{0:T(128)S(1)}, f32[2]{0:T(128)}, u32[]{:S(2)}) copy-start(f32[2]{0:T(128)} %add_convert_fusion) | copy-start | bytes 28
  43.0 31.5 %copy-start.2 = (f32[512]{0:T(512)S(1)}, f32[512]{0:T(512)}, u32[]{:S(2)}) copy-start(f32[512]{0:T(512)} %iota_convert_fusion) | copy-start | bytes 6148
  50.9 28.4 %collective-permute-start.3 = (f32[3,2,2048]{2,1,0:T(2,128)}, f32[3,2,2048]{2,1,0:T(2,128)}, u32[]{:S(2)}, u32[]{:S(2)}) collective-permute-start(f32[3,2,2048]{2,1,0:T(2,128)} %get-tuple-element.221), channel_id=1, source_target_pairs={{0,1},{1,2},{2,3},{3,4},{4,5},{5,6},{6,7},{8,9},{9,10},{10,11},{11... | collective-permute-start | bytes 147464 | tf_op jit(solution)/shard_map/ppermute | solution.py:17
  52.8 26.5 %collective-permute-start.4 = (f32[3,2,2048]{2,1,0:T(2,128)}, f32[3,2,2048]{2,1,0:T(2,128)}, u32[]{:S(2)}, u32[]{:S(2)}) collective-permute-start(f32[3,2,2048]{2,1,0:T(2,128)} %get-tuple-element.222), channel_id=1, source_target_pairs={{1,0},{2,1},{3,2},{4,3},{5,4},{6,5},{7,6},{9,8},{10,9},{11,10},{12... | collective-permute-start | bytes 147464 | tf_op jit(solution)/shard_map/ppermute | solution.py:20
  79.3 26.8 %copy-start.1 = (f32[4,2]{1,0:T(4,128)S(1)}, f32[4,2]{1,0:T(4,128)}, u32[]{:S(2)}) copy-start(f32[4,2]{1,0:T(4,128)} %constant.61.clone) | copy-start | bytes 100
  97.9 6.8 %collective-permute-start.5 = (f32[3,1,2048]{2,1,0:T(1,128)S(1)}, f32[3,1,2048]{2,1,0:T(1,128)S(1)}, u32[]{:S(2)}, u32[]{:S(2)}) collective-permute-start(f32[3,1,2048]{2,1,0:T(1,128)S(1)} %get-tuple-element.220), channel_id=1, source_target_pairs={{1,0},{2,1},{3,2},{4,3},{5,4},{6,5},{7,6},{9,8},{10,9},{11,10},{12... | collective-permute-start | bytes 73736 | tf_op jit(solution)/shard_map/ppermute | solution.py:20
  100.3 5.1 %collective-permute-start.6 = (f32[3,1,2048]{2,1,0:T(1,128)S(1)}, f32[3,1,2048]{2,1,0:T(1,128)S(1)}, u32[]{:S(2)}, u32[]{:S(2)}) collective-permute-start(f32[3,1,2048]{2,1,0:T(1,128)S(1)} %get-tuple-element.219), channel_id=1, source_target_pairs={{0,1},{1,2},{2,3},{3,4},{4,5},{5,6},{6,7},{8,9},{9,10},{10,11},{11... | collective-permute-start | bytes 73736 | tf_op jit(solution)/shard_map/ppermute | solution.py:17
  113.7 17.5 %collective-permute-start = (f32[4,2,8,2048]{3,2,1,0:T(8,128)S(1)}, f32[4,2,8,2048]{3,2,1,0:T(8,128)S(1)}, u32[]{:S(2)}, u32[]{:S(2)}) collective-permute-start(f32[4,2,8,2048]{3,2,1,0:T(8,128)S(1)} %pad_maximum_fusion.12), channel_id=1, source_target_pairs={{0,8},{8,16},{16,24},{1,9},{9,17},{17,25},{2,10},{10,18},{18,26},{... | collective-permute-start | bytes 1572872 | tf_op jit(solution)/shard_map/while/body/eval_jaxpr/ppermute | solution.py:28
  138.7 16.6 %collective-permute-start = (f32[4,2,8,2048]{3,2,1,0:T(8,128)S(1)}, f32[4,2,8,2048]{3,2,1,0:T(8,128)S(1)}, u32[]{:S(2)}, u32[]{:S(2)}) collective-permute-start(f32[4,2,8,2048]{3,2,1,0:T(8,128)S(1)} %pad_maximum_fusion.12), channel_id=1, source_target_pairs={{0,8},{8,16},{16,24},{1,9},{9,17},{17,25},{2,10},{10,18},{18,26},{... | collective-permute-start | bytes 1572872 | tf_op jit(solution)/shard_map/while/body/eval_jaxpr/ppermute | solution.py:28
  163.0 15.8 %collective-permute-start = (f32[4,2,8,2048]{3,2,1,0:T(8,128)S(1)}, f32[4,2,8,2048]{3,2,1,0:T(8,128)S(1)}, u32[]{:S(2)}, u32[]{:S(2)}) collective-permute-start(f32[4,2,8,2048]{3,2,1,0:T(8,128)S(1)} %pad_maximum_fusion.12), channel_id=1, source_target_pairs={{0,8},{8,16},{16,24},{1,9},{9,17},{17,25},{2,10},{10,18},{18,26},{... | collective-permute-start | bytes 1572872 | tf_op jit(solution)/shard_map/while/body/eval_jaxpr/ppermute | solution.py:28
where the time goes:
time: 188 us; the launch traced here: 187 us
  other arithmetic  56 us (30%)
  waiting for transfers between devices  42.8 us (23%)
  local copies, waits for them, and re-layouts  35.2 us (19%)
  starting transfers between devices  23.2 us (12%)
  blocking collectives  14.4 us (8%)
  matrix products  12.5 us (7%)
  between operations  2.16 us (1%)
    ppermute x3, waiting for transfers between devices, from_behind(): return lax.ppermute(value, axis, pairs)  42.1 us
    sub x12, other arithmetic, lens_step(): (1.0 - mixing) * previous + mixing * current - bending * bent_rows  26.3 us
    add x1, other arithmetic, body(): short_part + jnp.repeat(jnp.repeat(long_gain * jnp.einsum('pix,xy->piy',...  17.4 us
    all_gather x1, blocking collectives, body(): received = lax.all_gather(coarse, 'tile', axis=1, tiled=True)  14.4 us
    another operation x10, local copies, waits for them, and re-layouts, paint_rows(): jnp.stack([padded[..., 2 + 2 * row_step:2 + 2 * row_step + row_count, 2 +...  13.8 us
    ppermute x3, starting transfers between devices, extended_2(): lax.ppermute(lax.slice_in_dim(block, 0, width, axis=dim), axis, backward)  9.66 us
    reshape x1, local copies, waits for them, and re-layouts, body(): convergence.reshape(plane_count, coarse_here, 4, coarse_cols, 4)  7.88 us
    ppermute x3, starting transfers between devices, from_behind(): return lax.ppermute(value, axis, pairs)  7.8 us
  transfers between devices with their start and end apart: 9, of which 4 were waited for; matrix products, arithmetic and copies ran while one was open for 10% of the time, Pallas kernels for 0%

commit v1 on v0

v1 whole, which is shorter than its diff:
```python
import functools
import math

import jax
import jax.numpy as jnp
from jax import lax
from jax.experimental import pallas as pl
from jax.experimental.pallas import tpu as pltpu
from jax.sharding import PartitionSpec as P

lens_gain = 0.25
pad = 128
block = 512
f32 = jnp.float32
bf16 = jnp.bfloat16


def split(x):
    hi = x.astype(bf16)
    return hi, (x - hi.astype(f32)).astype(bf16)


def iota(shape, axis):
    return lax.broadcasted_iota(jnp.int32, shape, axis)


def dot(a, b):
    return jnp.dot(a, b, preferred_element_type=f32)


def kernel(
    tiles, groups, density, slot, weight, bias, mix, short, out,
    ext, conv, paint_lhs, short_lhs, col_hi, col_lo, spread, gathered, shorts, longs,
    halo_send, halo_recv, coarse_send, coarse_recv, short_send, short_recv, long_send, long_recv,
):
    planes, rows, cols = density.shape
    channels = weight.shape[0]
    slots = slot.shape[0]
    coarse_cols = cols // 4
    t = lax.axis_index("tile")
    g = lax.axis_index("plane")

    barrier = pltpu.get_barrier_semaphore()

    def greet_tile(j, carry):
        pl.semaphore_signal(barrier, inc=1, device_id={"tile": lax.rem(t + j, tiles)})
        return carry

    def greet_plane(j, carry):
        pl.semaphore_signal(barrier, inc=1, device_id={"plane": lax.rem(g + j, groups)})
        return carry

    lax.fori_loop(1, tiles, greet_tile, 0)
    lax.fori_loop(1, groups, greet_plane, 0)
    pl.semaphore_wait(barrier, tiles + groups - 2)

    def halo_copy(side):
        return pltpu.make_async_remote_copy(
            src_ref=density,
            dst_ref=ext.at[2 * side, :, :, pl.ds(pad, cols)],
            send_sem=halo_send.at[side],
            recv_sem=halo_recv.at[side],
            device_id={"tile": lax.rem(t + (1 if side == 0 else tiles - 1), tiles)},
        )

    has_low = t > 0
    has_high = t < tiles - 1

    @pl.when(has_high)
    def _():
        halo_copy(0).start()

    @pl.when(has_low)
    def _():
        halo_copy(1).start()

    ext[:, :, :, 0:pad] = jnp.zeros((3, planes, rows, pad), f32)
    ext[:, :, :, pad + cols :] = jnp.zeros((3, planes, rows, pad), f32)
    ext[1, :, :, pad : pad + cols] = density[...]
    conv[:, :, 0:pad] = jnp.zeros((planes, 16, pad), f32)
    conv[:, :, pad + cols :] = jnp.zeros((planes, 16, pad), f32)

    @pl.when(jnp.logical_not(has_low))
    def _():
        ext[0, :, :, pad : pad + cols] = jnp.zeros((planes, rows, cols), f32)

    @pl.when(jnp.logical_not(has_high))
    def _():
        ext[2, :, :, pad : pad + cols] = jnp.zeros((planes, rows, cols), f32)

    lane = iota((16, 240), 1)
    sub = iota((16, 240), 0)
    seg = jnp.where(lane >= 160, lane - 160, jnp.where(lane >= 80, lane - 80, lane))
    tap_masks = []
    for i in range(3):
        for j in range(3):
            tap_masks.append(seg == j * 24 + sub + 4 + 2 * (i - 1))

    def pack(value):
        hi = value.astype(bf16).astype(f32)
        return jnp.where(lane < 160, hi, value - hi).astype(bf16)

    def paint_channel(c, carry):
        value = jnp.zeros((16, 240), f32)
        for tap in range(9):
            value = jnp.where(tap_masks[tap], weight[c, tap], value)
        paint_lhs[pl.ds(pl.multiple_of(c * 16, 16), 16), :] = pack(value)
        return carry

    lax.fori_loop(0, channels, paint_channel, 0)

    row_of = jnp.where(sub < 8, sub, jnp.where(sub == 8, -1, 8))
    value = jnp.zeros((16, 240), f32)
    for a in range(5):
        for b in range(5):
            value = jnp.where(
                (seg == b * 16 + row_of + 2 + a) & (sub < 10), short[a, b], value
            )
    short_lhs[...] = pack(value)

    spread[...] = ((iota((128, block), 1) >> 2) == iota((128, block), 0)).astype(f32).astype(bf16)
    pool = ((iota((block, 128), 0) >> 2) == iota((block, 128), 1)).astype(f32).astype(bf16)
    col_scale = cols / 16.0

    def col_rows(i, carry):
        gap = iota((64, coarse_cols), 0) + i * 64 - iota((64, coarse_cols), 1)
        hi, lo = split(jnp.exp(-jnp.abs(gap.astype(f32)) / col_scale))
        at = pl.ds(pl.multiple_of(i * 64, 64), 64)
        col_hi[at, :] = hi
        col_lo[at, :] = lo
        return carry

    lax.fori_loop(0, coarse_cols // 64, col_rows, 0)

    @pl.when(has_low)
    def _():
        halo_copy(0).wait_recv()

    @pl.when(has_high)
    def _():
        halo_copy(1).wait_recv()

    row_global = iota((16, block), 0) + (t * rows - 4)
    row_real = (row_global >= 0) & (row_global < tiles * rows)

    def paint(cb, carry):
        window = pl.ds(pl.multiple_of(cb * block, block), block + 2 * pad)
        sums = []
        for p in range(planes):
            parts = [ext[s, p, :, window] for s in range(3)]
            stacked = []
            for j in range(3):
                start = pad + 2 * (j - 1)
                stacked += [part[:, start : start + block] for part in parts]
            stacked.append(jnp.zeros((8, block), f32))
            hi, lo = split(jnp.concatenate(stacked, axis=0))
            pre = dot(paint_lhs[...], jnp.concatenate([hi, lo, hi], axis=0))
            total = jnp.zeros((16, block), f32)
            for c in range(channels):
                total += mix[c] * jnp.tanh(pre[16 * c : 16 * c + 16] + bias[c])
            total = jnp.where(row_real, total, 0.0)
            conv[p, :, pl.ds(pl.multiple_of(cb * block + pad, pad), block)] = total
            sums.append(jnp.sum(total[4:8], axis=0, keepdims=True))
            sums.append(jnp.sum(total[8:12], axis=0, keepdims=True))
        sums += [jnp.zeros((1, block), f32)] * (8 - 2 * planes)
        hi, lo = split(jnp.concatenate(sums, axis=0) * (1.0 / 16.0))
        coarse = dot(hi, pool) + dot(lo, pool)
        gathered[t, :, pl.ds(pl.multiple_of(cb * 128, 128), 128)] = coarse
        return carry

    lax.fori_loop(0, cols // block, paint, 0)

    def coarse_copy(j):
        return pltpu.make_async_remote_copy(
            src_ref=gathered.at[t],
            dst_ref=gathered.at[t],
            send_sem=coarse_send.at[j],
            recv_sem=coarse_recv.at[t],
            device_id={"tile": lax.rem(t + j, tiles)},
        )

    def coarse_start(j, carry):
        coarse_copy(j).start()
        return carry

    lax.fori_loop(1, tiles, coarse_start, 0)

    def short_block(cb, carry):
        window = pl.ds(pl.multiple_of(cb * block, block), block + 2 * pad)
        at = pl.ds(pl.multiple_of(cb * block, block), block)
        edges = []
        for p in range(planes):
            part = conv[p, :, window]
            stacked = [part[:, pad + b - 2 : pad + b - 2 + block] for b in range(5)]
            hi, lo = split(jnp.concatenate(stacked, axis=0))
            value = dot(short_lhs[...], jnp.concatenate([hi, lo, hi], axis=0))
            shorts[g, p, :, at] = value[0:8]
            edges.append(value[8:10])
        edges += [jnp.zeros((8 - 2 * planes, block), f32)]
        shorts[g, planes, :, at] = jnp.concatenate(edges, axis=0)
        return carry

    lax.fori_loop(0, cols // block, short_block, 0)

    def later_copy(buffer, send, recv, to):
        return pltpu.make_async_remote_copy(
            src_ref=buffer.at[g],
            dst_ref=buffer.at[g],
            send_sem=send.at[to],
            recv_sem=recv.at[g],
            device_id={"plane": to},
        )

    def short_start(to, carry):
        later_copy(shorts, short_send, short_recv, to).start()
        return carry

    lax.fori_loop(g + 1, groups, short_start, 0)

    def coarse_wait(j, carry):
        source = lax.rem(t + j, tiles)
        pltpu.make_async_remote_copy(
            src_ref=gathered.at[source],
            dst_ref=gathered.at[source],
            send_sem=coarse_send.at[j],
            recv_sem=coarse_recv.at[source],
            device_id={"tile": source},
        ).wait_recv()
        return carry

    lax.fori_loop(1, tiles, coarse_wait, 0)
    row_scale = tiles * rows / 16.0
    long_gain = 1.0 / math.sqrt(row_scale * col_scale)
    m = iota((16, tiles * 8), 0)
    n = iota((16, tiles * 8), 1)
    gap = (2 * t - 1 + (m & 3)) - (2 * (n >> 3) + (n & 1))
    near = jnp.exp(-jnp.abs(gap.astype(f32)) / row_scale) * long_gain
    row_kernel = jnp.where((m >> 2) == ((n & 7) >> 1), near, 0.0)
    everything = gathered[...].reshape(tiles * 8, coarse_cols)
    summed = jnp.dot(
        row_kernel, everything, preferred_element_type=f32, precision=lax.Precision.HIGHEST
    )
    hi, lo = split(summed)
    longs[g] = dot(hi, col_hi[...]) + dot(lo, col_hi[...]) + dot(hi, col_lo[...])

    def long_start(to, carry):
        later_copy(longs, long_send, long_recv, to).start()
        return carry

    lax.fori_loop(g + 1, groups, long_start, 0)

    for entry in range(4):
        for p in (planes - 2, planes - 1):
            out[entry, p] = jnp.full((rows, cols), 1.0 if entry in (0, 3) else 0.0, f32)
    row_at = iota((rows, cols), 0)
    col_at = iota((rows, cols), 1)
    low_gain = jnp.where(t > 0, 1.0, 0.0)
    high_gain = jnp.where(t < tiles - 1, 1.0, 0.0)
    slot_total = 2.0 * slots
    wide = cols // 128

    def next_col(x):
        return jnp.where(col_at == cols - 1, 0.0, pltpu.roll(x, cols - 1, 1))

    def last_col(x):
        return jnp.where(col_at == 0, 0.0, pltpu.roll(x, 1, 1))

    def lens(gi, carry):
        @pl.when(gi < g)
        def _():
            for buffer, send, recv in (
                (shorts, short_send, short_recv), (longs, long_send, long_recv)
            ):
                pltpu.make_async_remote_copy(
                    src_ref=buffer.at[gi],
                    dst_ref=buffer.at[gi],
                    send_sem=send.at[gi],
                    recv_sem=recv.at[gi],
                    device_id={"plane": gi},
                ).wait_recv()

        hi, lo = split(longs[gi])
        pieces = coarse_cols // 128
        stacked = [x[:, 128 * b : 128 * b + 128] for x in (hi, lo) for b in range(pieces)]
        spread_out = dot(jnp.concatenate(stacked, axis=0), spread[...])
        upper = [
            spread_out[16 * b : 16 * b + 16]
            + spread_out[16 * (pieces + b) : 16 * (pieces + b) + 16]
            for b in range(pieces)
        ]
        long_wide = jnp.concatenate(upper, axis=1)
        edges = shorts[gi, planes]
        for p in range(planes):
            k = gi * planes + p

            def distance(index):
                value = jnp.full((8, 128), slot[index], jnp.int32)
                return (value.astype(f32) + 1.0) / slot_total

            here = distance(k)
            before = jnp.where(k > 0, distance(jnp.maximum(k - 1, 0)), 0.0)
            after = jnp.where(
                k < slots - 1,
                distance(jnp.minimum(k + 1, slots - 1)),
                (slot_total + 1.0) / slot_total,
            )
            mixing = before * (after - here) / (here * (after - before))
            bending = lens_gain * (after - here) / after
            mixing = jnp.concatenate([mixing] * wide, axis=1)
            bending = jnp.concatenate([bending] * wide, axis=1)
            center = shorts[gi, p] + jnp.where(
                row_at < 4, long_wide[4 * p + 1 : 4 * p + 2], long_wide[4 * p + 2 : 4 * p + 3]
            )
            top = (edges[2 * p : 2 * p + 1] + long_wide[4 * p : 4 * p + 1]) * low_gain
            bottom = (
                edges[2 * p + 1 : 2 * p + 2] + long_wide[4 * p + 3 : 4 * p + 4]
            ) * high_gain
            up = jnp.where(row_at == 0, top, pltpu.roll(center, 1, 0))
            down = jnp.where(row_at == rows - 1, bottom, pltpu.roll(center, rows - 1, 0))
            u11 = (down - 2.0 * center + up) * bending
            u22 = (next_col(center) - 2.0 * center + last_col(center)) * bending
            slope = down - up
            u12 = (next_col(slope) - last_col(slope)) * (0.25 * bending)
            old = [out[e, (p - 2) % planes] for e in range(4)]
            new = [out[e, (p - 1) % planes] for e in range(4)]
            bent = [
                u11 * new[0] + u12 * new[2],
                u11 * new[1] + u12 * new[3],
                u12 * new[0] + u22 * new[2],
                u12 * new[1] + u22 * new[3],
            ]
            for e in range(4):
                out[e, p] = (1.0 - mixing) * old[e] + mixing * new[e] - bent[e]
        return carry

    lax.fori_loop(0, g + 1, lens, 0)

    @pl.when(has_high)
    def _():
        halo_copy(0).wait_send()

    @pl.when(has_low)
    def _():
        halo_copy(1).wait_send()

    def coarse_sent(j, carry):
        coarse_copy(j).wait_send()
        return carry

    lax.fori_loop(1, tiles, coarse_sent, 0)

    def later_sent(to, carry):
        later_copy(shorts, short_send, short_recv, to).wait_send()
        later_copy(longs, long_send, long_recv, to).wait_send()
        return carry

    lax.fori_loop(g + 1, groups, later_sent, 0)


def solution(mesh):
    tiles, groups = mesh.shape["tile"], mesh.shape["plane"]

    def body(density, plane_slot, paint_weight, paint_bias, mix_weight, short_kernel):
        planes, rows, cols = density.shape
        channels = paint_weight.shape[0]
        coarse_cols = cols // 4
        vmem = pl.BlockSpec(memory_space=pltpu.VMEM)
        smem = pl.BlockSpec(memory_space=pltpu.SMEM)
        wide = cols + 2 * pad
        dma = pltpu.SemaphoreType.DMA
        return pl.pallas_call(
            functools.partial(kernel, tiles, groups),
            out_shape=jax.ShapeDtypeStruct((4, planes, rows, cols), f32),
            in_specs=[vmem] + [smem] * 5,
            out_specs=vmem,
            scratch_shapes=[
                pltpu.VMEM((3, planes, rows, wide), f32),
                pltpu.VMEM((planes, 16, wide), f32),
                pltpu.VMEM((16 * channels, 240), bf16),
                pltpu.VMEM((16, 240), bf16),
                pltpu.VMEM((coarse_cols, coarse_cols), bf16),
                pltpu.VMEM((coarse_cols, coarse_cols), bf16),
                pltpu.VMEM((128, block), bf16),
                pltpu.VMEM((tiles, 8, coarse_cols), f32),
                pltpu.VMEM((groups, planes + 1, rows, cols), f32),
                pltpu.VMEM((groups, 16, coarse_cols), f32),
                dma((2,)),
                dma((2,)),
                dma((tiles,)),
                dma((tiles,)),
                dma((groups,)),
                dma((groups,)),
                dma((groups,)),
                dma((groups,)),
            ],
            compiler_params=pltpu.CompilerParams(
                collective_id=0, has_side_effects=True, vmem_limit_bytes=48 * 1024 * 1024
            ),
        )(density, plane_slot, paint_weight, paint_bias, mix_weight, short_kernel)

    placed = (P("plane", "tile", None), P(), P(), P(), P(), P())
    return jax.shard_map(
        body, mesh=mesh, in_specs=placed, out_specs=P(None, "plane", "tile", None), check_vma=False
    )
```

time: 188 us -> 34.1 us (0.18)
  the two profiles are of different devices: /device:TPU:12 before, /device:TPU:15 now
where the time goes in v1:
time: 34.1 us; the launch traced here: 33.9 us
  Pallas kernels  31.2 us (91%)
  local copies, waits for them, and re-layouts  2.64 us (8%)
    pallas_call x1, Pallas kernels, body(): pl.pallas_call(functools.partial(kernel, tiles, groups), out_shape=jax.Sh...  31.2 us
    unnamed x12, local copies, waits for them, and re-layouts  2.64 us

profile of v1, /device:TPU:15, one launch (start us, length us, event | category | flops | bytes accessed | tf_op | source)
XLA Modules:
  0.0 33.9 jit_solution(3308539656142089003)
XLA Ops:
  0.0 0.0 copy-start.1
  0.0 0.0 copy-start.4
  0.0 0.0 copy-start.3
  0.0 0.0 copy-start.2
  0.0 0.8 %copy.7.weight = f32[32,9]{1,0:T(8,128)S(1)} copy(f32[32,9]{0,1:T(8,128)} %param.8) | data formatting | bytes 2304 | tf_op args[2]
  0.8 0.0 copy-done.1
  0.8 0.0 copy-done.4
  0.8 0.0 copy-done.3
  0.9 0.0 copy-done.2
  0.9 0.0 copy-start
  0.9 0.9 %copy-done = f32[3,8,2048]{2,1,0:T(8,128)S(1)} copy-done((f32[3,8,2048]{2,1,0:T(8,128)S(1)}, f32[3,8,2048]{2,1,0:T(8,128)}, u32[]{:S(2)}) %copy-start) | copy-done | bytes 196632
  1.8 31.2 %shard_map.64 = f32[4,3,8,2048]{3,2,1,0:T(8,128)S(1)} custom-call(f32[3,8,2048]{2,1,0:T(8,128)S(1)} %copy-done, s32[12]{0:T(128)S(1)} %copy-done.2, f32[32,9]{1,0:T(8,128)S(1)} %copy.7.weight, f32[32]{0:T(128)S(1)} %copy-done.3, f32[32]{0:T(128)S(1)} %copy-done.4, f32[5,5]{1,0:T(8,128)S(1)} %copy-done.1), custom_call_target="tpu_custom_call" | custom-call | tf_op jit(solution)/shard_map/pallas_call | solution.py:371
  33.1 0.9 %copy.9 = f32[4,3,8,2048]{3,2,1,0:T(8,128)} copy(f32[4,3,8,2048]{3,2,1,0:T(8,128)S(1)} %shard_map.64) | data formatting | bytes 1572864
Async XLA Ops:
  0.0 0.8 %copy-start.1 = (f32[5,5]{1,0:T(8,128)S(1)}, f32[5,5]{1,0:T(8,128)}, u32[]{:S(2)}) copy-start(f32[5,5]{1,0:T(8,128)} %short.1) | copy-start | bytes 304
  0.0 0.8 %copy-start.4 = (f32[32]{0:T(128)S(1)}, f32[32]{0:T(128)}, u32[]{:S(2)}) copy-start(f32[32]{0:T(128)} %mix.1) | copy-start | bytes 388
  0.0 0.8 %copy-start.3 = (f32[32]{0:T(128)S(1)}, f32[32]{0:T(128)}, u32[]{:S(2)}) copy-start(f32[32]{0:T(128)} %bias.1) | copy-start | bytes 388
  0.0 0.8 %copy-start.2 = (s32[12]{0:T(128)S(1)}, s32[12]{0:T(128)}, u32[]{:S(2)}) copy-start(s32[12]{0:T(128)} %slot.1) | copy-start | bytes 148
  0.9 0.9 %copy-start = (f32[3,8,2048]{2,1,0:T(8,128)S(1)}, f32[3,8,2048]{2,1,0:T(8,128)}, u32[]{:S(2)}) copy-start(f32[3,8,2048]{2,1,0:T(8,128)} %density.1) | copy-start | bytes 589828

commit v2 on v1

--- a/solution.py
+++ b/solution.py
@@ -31,15 +31,19 @@
 def kernel(
     tiles, groups, density, slot, weight, bias, mix, short, out,
     ext, conv, paint_lhs, short_lhs, col_hi, col_lo, spread, gathered, shorts, longs,
-    halo_send, halo_recv, coarse_send, coarse_recv, short_send, short_recv, long_send, long_recv,
+    own_sem, halo_send, halo_recv, coarse_send, coarse_recv, short_send, short_recv, long_send, long_recv,
 ):
     planes, rows, cols = density.shape
-    channels = weight.shape[0]
+    channels = weight.shape[1]
+    blocks = cols // block
     slots = slot.shape[0]
     coarse_cols = cols // 4
     t = lax.axis_index("tile")
     g = lax.axis_index("plane")
 
+    own_copy = pltpu.make_async_copy(density, ext.at[1, :, :, pl.ds(pad, cols)], own_sem)
+    own_copy.start()
+
     barrier = pltpu.get_barrier_semaphore()
 
     def greet_tile(j, carry):
@@ -54,29 +58,34 @@
     lax.fori_loop(1, groups, greet_plane, 0)
     pl.semaphore_wait(barrier, tiles + groups - 2)
 
-    def halo_copy(side):
+    def halo_copy(side, cb):
+        start = pl.multiple_of(cb * block, block)
         return pltpu.make_async_remote_copy(
-            src_ref=density,
-            dst_ref=ext.at[2 * side, :, :, pl.ds(pad, cols)],
-            send_sem=halo_send.at[side],
-            recv_sem=halo_recv.at[side],
+            src_ref=density.at[:, :, pl.ds(start, block)],
+            dst_ref=ext.at[2 * side, :, :, pl.ds(pl.multiple_of(start + pad, pad), block)],
+            send_sem=halo_send.at[side, cb],
+            recv_sem=halo_recv.at[side, cb],
             device_id={"tile": lax.rem(t + (1 if side == 0 else tiles - 1), tiles)},
         )
 
     has_low = t > 0
     has_high = t < tiles - 1
 
-    @pl.when(has_high)
-    def _():
-        halo_copy(0).start()
-
-    @pl.when(has_low)
-    def _():
-        halo_copy(1).start()
+    def halo_start(cb, carry):
+        @pl.when(has_high)
+        def _():
+            halo_copy(0, cb).start()
+
+        @pl.when(has_low)
+        def _():
+            halo_copy(1, cb).start()
+
+        return carry
+
+    lax.fori_loop(0, blocks, halo_start, 0)
 
     ext[:, :, :, 0:pad] = jnp.zeros((3, planes, rows, pad), f32)
     ext[:, :, :, pad + cols :] = jnp.zeros((3, planes, rows, pad), f32)
-    ext[1, :, :, pad : pad + cols] = density[...]
     conv[:, :, 0:pad] = jnp.zeros((planes, 16, pad), f32)
     conv[:, :, pad + cols :] = jnp.zeros((planes, 16, pad), f32)
 
@@ -103,7 +112,7 @@
     def paint_channel(c, carry):
         value = jnp.zeros((16, 240), f32)
         for tap in range(9):
-            value = jnp.where(tap_masks[tap], weight[c, tap], value)
+            value = jnp.where(tap_masks[tap], weight[tap, c], value)
         paint_lhs[pl.ds(pl.multiple_of(c * 16, 16), 16), :] = pack(value)
         return carry
 
@@ -132,18 +141,22 @@
 
     lax.fori_loop(0, coarse_cols // 64, col_rows, 0)
 
-    @pl.when(has_low)
-    def _():
-        halo_copy(0).wait_recv()
-
-    @pl.when(has_high)
-    def _():
-        halo_copy(1).wait_recv()
+    def halo_wait(cb):
+        @pl.when(has_low)
+        def _():
+            halo_copy(0, cb).wait_recv()
+
+        @pl.when(has_high)
+        def _():
+            halo_copy(1, cb).wait_recv()
+
+    own_copy.wait()
+    halo_wait(0)
 
     row_global = iota((16, block), 0) + (t * rows - 4)
     row_real = (row_global >= 0) & (row_global < tiles * rows)
 
-    def paint(cb, carry):
+    def paint(cb):
         window = pl.ds(pl.multiple_of(cb * block, block), block + 2 * pad)
         sums = []
         for p in range(planes):
@@ -166,26 +179,27 @@
         hi, lo = split(jnp.concatenate(sums, axis=0) * (1.0 / 16.0))
         coarse = dot(hi, pool) + dot(lo, pool)
         gathered[t, :, pl.ds(pl.multiple_of(cb * 128, 128), 128)] = coarse
-        return carry
-
-    lax.fori_loop(0, cols // block, paint, 0)
-
-    def coarse_copy(j):
+
+    def short_copy(cb, to):
+        at = pl.ds(pl.multiple_of(cb * block, block), block)
         return pltpu.make_async_remote_copy(
-            src_ref=gathered.at[t],
-            dst_ref=gathered.at[t],
-            send_sem=coarse_send.at[j],
-            recv_sem=coarse_recv.at[t],
-            device_id={"tile": lax.rem(t + j, tiles)},
+            src_ref=shorts.at[g, :, :, at],
+            dst_ref=shorts.at[g, :, :, at],
+            send_sem=short_send.at[to, cb],
+            recv_sem=short_recv.at[g, cb],
+            device_id={"plane": to},
         )
 
-    def coarse_start(j, carry):
-        coarse_copy(j).start()
-        return carry
-
-    lax.fori_loop(1, tiles, coarse_start, 0)
-
-    def short_block(cb, carry):
+    def long_copy(to):
+        return pltpu.make_async_remote_copy(
+            src_ref=longs.at[g],
+            dst_ref=longs.at[g],
+            send_sem=long_send.at[to],
+            recv_sem=long_recv.at[g],
+            device_id={"plane": to},
+        )
+
+    def short_block(cb):
         window = pl.ds(pl.multiple_of(cb * block, block), block + 2 * pad)
         at = pl.ds(pl.multiple_of(cb * block, block), block)
         edges = []
@@ -198,24 +212,42 @@
             edges.append(value[8:10])
         edges += [jnp.zeros((8 - 2 * planes, block), f32)]
         shorts[g, planes, :, at] = jnp.concatenate(edges, axis=0)
-        return carry
-
-    lax.fori_loop(0, cols // block, short_block, 0)
-
-    def later_copy(buffer, send, recv, to):
+
+        def short_start(to, carry):
+            short_copy(cb, to).start()
+            return carry
+
+        lax.fori_loop(g + 1, groups, short_start, 0)
+
+    def coarse_copy(j):
         return pltpu.make_async_remote_copy(
-            src_ref=buffer.at[g],
-            dst_ref=buffer.at[g],
-            send_sem=send.at[to],
-            recv_sem=recv.at[g],
-            device_id={"plane": to},
+            src_ref=gathered.at[t],
+            dst_ref=gathered.at[t],
+            send_sem=coarse_send.at[j],
+            recv_sem=coarse_recv.at[t],
+            device_id={"tile": lax.rem(t + j, tiles)},
         )
 
-    def short_start(to, carry):
-        later_copy(shorts, short_send, short_recv, to).start()
-        return carry
-
-    lax.fori_loop(g + 1, groups, short_start, 0)
+    def coarse_start(j, carry):
+        coarse_copy(j).start()
+        return carry
+
+    def paint_step(cb, carry):
+        @pl.when(cb + 1 < blocks)
+        def _():
+            halo_wait(cb + 1)
+
+        paint(cb)
+
+        @pl.when(cb > 0)
+        def _():
+            short_block(cb - 1)
+
+        return carry
+
+    lax.fori_loop(0, blocks, paint_step, 0)
+    lax.fori_loop(1, tiles, coarse_start, 0)
+    short_block(blocks - 1)
 
     def coarse_wait(j, carry):
         source = lax.rem(t + j, tiles)
@@ -237,14 +269,17 @@
     near = jnp.exp(-jnp.abs(gap.astype(f32)) / row_scale) * long_gain
     row_kernel = jnp.where((m >> 2) == ((n & 7) >> 1), near, 0.0)
     everything = gathered[...].reshape(tiles * 8, coarse_cols)
-    summed = jnp.dot(
-        row_kernel, everything, preferred_element_type=f32, precision=lax.Precision.HIGHEST
+    row_hi, row_lo = split(row_kernel)
+    hi, lo = split(everything)
+    summed = dot(
+        jnp.concatenate([row_hi, row_hi, row_lo], axis=1), jnp.concatenate([hi, lo, hi], axis=0)
     )
     hi, lo = split(summed)
-    longs[g] = dot(hi, col_hi[...]) + dot(lo, col_hi[...]) + dot(hi, col_lo[...])
+    both = dot(jnp.concatenate([hi, lo], axis=0), col_hi[...])
+    longs[g] = both[0:16] + both[16:32] + dot(hi, col_lo[...])
 
     def long_start(to, carry):
-        later_copy(longs, long_send, long_recv, to).start()
+        long_copy(to).start()
         return carry
 
     lax.fori_loop(g + 1, groups, long_start, 0)
@@ -268,16 +303,25 @@
     def lens(gi, carry):
         @pl.when(gi < g)
         def _():
-            for buffer, send, recv in (
-                (shorts, short_send, short_recv), (longs, long_send, long_recv)
-            ):
+            def short_wait(cb, carry):
+                at = pl.ds(pl.multiple_of(cb * block, block), block)
                 pltpu.make_async_remote_copy(
-                    src_ref=buffer.at[gi],
-                    dst_ref=buffer.at[gi],
-                    send_sem=send.at[gi],
-                    recv_sem=recv.at[gi],
+                    src_ref=shorts.at[gi, :, :, at],
+                    dst_ref=shorts.at[gi, :, :, at],
+                    send_sem=short_send.at[gi, cb],
+                    recv_sem=short_recv.at[gi, cb],
                     device_id={"plane": gi},
                 ).wait_recv()
+                return carry
+
+            lax.fori_loop(0, blocks, short_wait, 0)
+            pltpu.make_async_remote_copy(
+                src_ref=longs.at[gi],
+                dst_ref=longs.at[gi],
+                send_sem=long_send.at[gi],
+                recv_sem=long_recv.at[gi],
+                device_id={"plane": gi},
+            ).wait_recv()
 
         hi, lo = split(longs[gi])
         pieces = coarse_cols // 128
@@ -335,13 +379,18 @@
 
     lax.fori_loop(0, g + 1, lens, 0)
 
-    @pl.when(has_high)
-    def _():
-        halo_copy(0).wait_send()
-
-    @pl.when(has_low)
-    def _():
-        halo_copy(1).wait_send()
+    def halo_sent(cb, carry):
+        @pl.when(has_high)
+        def _():
+            halo_copy(0, cb).wait_send()
+
+        @pl.when(has_low)
+        def _():
+            halo_copy(1, cb).wait_send()
+
+        return carry
+
+    lax.fori_loop(0, blocks, halo_sent, 0)
 
     def coarse_sent(j, carry):
         coarse_copy(j).wait_send()
@@ -350,8 +399,12 @@
     lax.fori_loop(1, tiles, coarse_sent, 0)
 
     def later_sent(to, carry):
-        later_copy(shorts, short_send, short_recv, to).wait_send()
-        later_copy(longs, long_send, long_recv, to).wait_send()
+        def block_sent(cb, inner):
+            short_copy(cb, to).wait_send()
+            return inner
+
+        lax.fori_loop(0, blocks, block_sent, 0)
+        long_copy(to).wait_send()
         return carry
 
     lax.fori_loop(g + 1, groups, later_sent, 0)
@@ -364,6 +417,7 @@
         planes, rows, cols = density.shape
         channels = paint_weight.shape[0]
         coarse_cols = cols // 4
+        blocks = cols // block
         vmem = pl.BlockSpec(memory_space=pltpu.VMEM)
         smem = pl.BlockSpec(memory_space=pltpu.SMEM)
         wide = cols + 2 * pad
@@ -371,7 +425,7 @@
         return pl.pallas_call(
             functools.partial(kernel, tiles, groups),
             out_shape=jax.ShapeDtypeStruct((4, planes, rows, cols), f32),
-            in_specs=[vmem] + [smem] * 5,
+            in_specs=[pl.BlockSpec(memory_space=pltpu.HBM)] + [smem] * 5,
             out_specs=vmem,
             scratch_shapes=[
                 pltpu.VMEM((3, planes, rows, wide), f32),
@@ -384,19 +438,20 @@
                 pltpu.VMEM((tiles, 8, coarse_cols), f32),
                 pltpu.VMEM((groups, planes + 1, rows, cols), f32),
                 pltpu.VMEM((groups, 16, coarse_cols), f32),
-                dma((2,)),
-                dma((2,)),
+                dma(()),
+                dma((2, blocks)),
+                dma((2, blocks)),
                 dma((tiles,)),
                 dma((tiles,)),
-                dma((groups,)),
-                dma((groups,)),
+                dma((groups, blocks)),
+                dma((groups, blocks)),
                 dma((groups,)),
                 dma((groups,)),
             ],
             compiler_params=pltpu.CompilerParams(
                 collective_id=0, has_side_effects=True, vmem_limit_bytes=48 * 1024 * 1024
             ),
-        )(density, plane_slot, paint_weight, paint_bias, mix_weight, short_kernel)
+        )(density, plane_slot, paint_weight.T, paint_bias, mix_weight, short_kernel)
 
     placed = (P("plane", "tile", None), P(), P(), P(), P(), P())
     return jax.shard_map(

time: 34.1 us -> 31.8 us (0.933)
  Pallas kernels: 31.2 us -> 27.7 us
  local copies, waits for them, and re-layouts: 2.64 us -> 3.87 us
    pallas_call x1, Pallas kernels: 31.2 us -> 27.7 us  [body(): pl.pallas_call(functools.partial(kernel, tiles, groups), out_shape=jax.Sh...]
    unnamed x12 -> x13, local copies, waits for them, and re-layouts: 2.64 us -> 3.87 us
where the time goes in v2:
time: 31.8 us; the launch traced here: 31.6 us
  Pallas kernels  27.7 us (87%)
  local copies, waits for them, and re-layouts  3.87 us (12%)
    pallas_call x1, Pallas kernels, body(): pl.pallas_call(functools.partial(kernel, tiles, groups), out_shape=jax.Sh...  27.7 us
    unnamed x13, local copies, waits for them, and re-layouts  3.87 us

profile of v2, /device:TPU:15, one launch (start us, length us, event | category | flops | bytes accessed | tf_op | source)
XLA Modules:
  0.0 31.6 jit_solution(18074533861376555056)
XLA Ops:
  0.0 0.0 copy-start.5
  0.0 0.0 copy-start.4
  0.0 0.0 copy-start.3
  0.0 0.6 %copy-done.5 = f32[32]{0:T(128)S(1)} copy-done((f32[32]{0:T(128)S(1)}, f32[32]{0:T(128)}, u32[]{:S(2)}) %copy-start.5) | copy-done | bytes 152
  0.7 0.0 copy-done.4
  0.7 0.0 copy-done.3
  0.7 0.0 copy-start
  0.7 0.9 %copy-done = f32[3,8,2048]{2,1,0:T(8,128)S(1)} copy-done((f32[3,8,2048]{2,1,0:T(8,128)S(1)}, f32[3,8,2048]{2,1,0:T(8,128)}, u32[]{:S(2)}) %copy-start) | copy-done | bytes 196632
  1.6 0.0 copy-start.1
  1.6 0.7 %copy-done.1 = f32[32,9]{0,1:T(8,128)S(1)} copy-done((f32[32,9]{0,1:T(8,128)S(1)}, f32[32,9]{0,1:T(8,128)}, u32[]{:S(2)}) %copy-start.1) | copy-done | bytes 1176
  2.3 0.0 copy-start.2
  2.3 0.7 %copy-done.2 = f32[5,5]{1,0:T(8,128)S(1)} copy-done((f32[5,5]{1,0:T(8,128)S(1)}, f32[5,5]{1,0:T(8,128)}, u32[]{:S(2)}) %copy-start.2) | copy-done | bytes 124
  3.0 27.7 %shard_map.64 = f32[4,3,8,2048]{3,2,1,0:T(8,128)S(1)} custom-call(f32[3,8,2048]{2,1,0:T(8,128)S(1)} %copy-done, s32[12]{0:T(128)S(1)} %copy-done.3, f32[9,32]{1,0:T(8,128)S(1)} %bitcast.1, f32[32]{0:T(128)S(1)} %copy-done.4, f32[32]{0:T(128)S(1)} %copy-done.5, f32[5,5]{1,0:T(8,128)S(1)} %copy-done.2), custom_call_target="tpu_custom_call" | custom-call | tf_op jit(solution)/shard_map/pallas_call | solution.py:425
  30.7 0.9 %copy.8 = f32[4,3,8,2048]{3,2,1,0:T(8,128)} copy(f32[4,3,8,2048]{3,2,1,0:T(8,128)S(1)} %shard_map.64) | data formatting | bytes 1572864
Async XLA Ops:
  0.0 0.7 %copy-start.5 = (f32[32]{0:T(128)S(1)}, f32[32]{0:T(128)}, u32[]{:S(2)}) copy-start(f32[32]{0:T(128)} %mix.1) | copy-start | bytes 388
  0.0 0.7 %copy-start.4 = (f32[32]{0:T(128)S(1)}, f32[32]{0:T(128)}, u32[]{:S(2)}) copy-start(f32[32]{0:T(128)} %bias.1) | copy-start | bytes 388
  0.0 0.7 %copy-start.3 = (s32[12]{0:T(128)S(1)}, s32[12]{0:T(128)}, u32[]{:S(2)}) copy-start(s32[12]{0:T(128)} %slot.1) | copy-start | bytes 148
  0.7 0.9 %copy-start = (f32[3,8,2048]{2,1,0:T(8,128)S(1)}, f32[3,8,2048]{2,1,0:T(8,128)}, u32[]{:S(2)}) copy-start(f32[3,8,2048]{2,1,0:T(8,128)} %density.1) | copy-start | bytes 589828
  1.6 0.7 %copy-start.1 = (f32[32,9]{0,1:T(8,128)S(1)}, f32[32,9]{0,1:T(8,128)}, u32[]{:S(2)}) copy-start(f32[32,9]{0,1:T(8,128)} %param.8) | copy-start | bytes 3460
  2.3 0.7 %copy-start.2 = (f32[5,5]{1,0:T(8,128)S(1)}, f32[5,5]{1,0:T(8,128)}, u32[]{:S(2)}) copy-start(f32[5,5]{1,0:T(8,128)} %short.1) | copy-start | bytes 304

commit v3 on v2

v3 whole, which is shorter than its diff:
```python
import functools
import math

import jax
import jax.numpy as jnp
from jax import lax
from jax.experimental import pallas as pl
from jax.experimental.pallas import tpu as pltpu
from jax.sharding import PartitionSpec as P

lens_gain = 0.25
pad = 128
block = 512
f32 = jnp.float32
bf16 = jnp.bfloat16


def split(x):
    hi = x.astype(bf16)
    return hi, (x - hi.astype(f32)).astype(bf16)


def iota(shape, axis):
    return lax.broadcasted_iota(jnp.int32, shape, axis)


def dot(a, b):
    return jnp.dot(a, b, preferred_element_type=f32)


def kernel(
    tiles, groups, density, slot, weight, bias, mix, short, out,
    mass_own, mass_edge, conv_own, conv_edge, paint_lhs, short_lhs, col_hi, col_lo, spread,
    gathered, shorts, longs, long_wide, state,
    own_sem, out_sem, mass_send, mass_recv, conv_send, conv_recv, coarse_send, coarse_recv,
    short_send, short_recv, long_send, long_recv,
):
    planes, rows, cols = density.shape
    channels = weight.shape[1]
    blocks = cols // block
    slots = slot.shape[0]
    coarse_cols = cols // 4
    half = rows // 2
    t = lax.axis_index("tile")
    g = lax.axis_index("plane")
    has_low = t > 0
    has_high = t < tiles - 1

    def at_block(cb):
        return pl.ds(pl.multiple_of(cb * block, block), block)

    def at_padded(cb):
        return pl.ds(pl.multiple_of(cb * block + pad, pad), block)

    def at_window(cb):
        return pl.ds(pl.multiple_of(cb * block, block), block + 2 * pad)

    own_copy = pltpu.make_async_copy(density, mass_own.at[:, :, pl.ds(pad, cols)], own_sem)
    own_copy.start()

    barrier = pltpu.get_barrier_semaphore()

    def greet_tile(j, carry):
        pl.semaphore_signal(barrier, inc=1, device_id={"tile": lax.rem(t + j, tiles)})
        return carry

    def greet_plane(j, carry):
        pl.semaphore_signal(barrier, inc=1, device_id={"plane": lax.rem(g + j, groups)})
        return carry

    lax.fori_loop(1, tiles, greet_tile, 0)
    lax.fori_loop(1, groups, greet_plane, 0)
    pl.semaphore_wait(barrier, tiles + groups - 2)

    def edge_copy(source, source_at, target, send, recv, side, cb):
        take = pl.ds(half, half) if side == 0 else pl.ds(0, half)
        give = pl.ds(0, half) if side == 0 else pl.ds(half, half)
        return pltpu.make_async_remote_copy(
            src_ref=source.at[:, take, source_at(cb)],
            dst_ref=target.at[:, give, at_padded(cb)],
            send_sem=send.at[side, cb],
            recv_sem=recv.at[side, cb],
            device_id={"tile": lax.rem(t + (1 if side == 0 else tiles - 1), tiles)},
        )

    def mass_copy(side, cb):
        return edge_copy(density, at_block, mass_edge, mass_send, mass_recv, side, cb)

    def conv_copy(side, cb):
        return edge_copy(conv_own, at_padded, conv_edge, conv_send, conv_recv, side, cb)

    def edge_start(copy, cb):
        @pl.when(has_high)
        def _():
            copy(0, cb).start()

        @pl.when(has_low)
        def _():
            copy(1, cb).start()

    def edge_wait(copy, cb):
        @pl.when(has_low)
        def _():
            copy(0, cb).wait_recv()

        @pl.when(has_high)
        def _():
            copy(1, cb).wait_recv()

    def edge_sent(copy, cb):
        @pl.when(has_high)
        def _():
            copy(0, cb).wait_send()

        @pl.when(has_low)
        def _():
            copy(1, cb).wait_send()

    def mass_start(cb, carry):
        edge_start(mass_copy, cb)
        return carry

    lax.fori_loop(0, blocks, mass_start, 0)

    for buffer in (mass_own, mass_edge, conv_own, conv_edge):
        buffer[:, :, 0:pad] = jnp.zeros((planes, rows, pad), f32)
        buffer[:, :, pad + cols :] = jnp.zeros((planes, rows, pad), f32)
    for buffer in (mass_edge, conv_edge):

        @pl.when(jnp.logical_not(has_low))
        def _():
            buffer[:, 0:half, pad : pad + cols] = jnp.zeros((planes, half, cols), f32)

        @pl.when(jnp.logical_not(has_high))
        def _():
            buffer[:, half:rows, pad : pad + cols] = jnp.zeros((planes, half, cols), f32)

    shorts[:, :, :, 0:pad] = jnp.zeros((groups, planes + 1, rows, pad), f32)
    shorts[:, :, :, pad + cols :] = jnp.zeros((groups, planes + 1, rows, pad), f32)
    long_wide[:, 0:pad] = jnp.zeros((16, pad), f32)
    long_wide[:, pad + cols :] = jnp.zeros((16, pad), f32)

    def row_of_place(place):
        return jnp.where(place < half, place - half, jnp.where(place < rows, place + half, place - rows))

    def pack(value, lane, size):
        hi = value.astype(bf16).astype(f32)
        return jnp.where(lane < 2 * size, hi, value - hi).astype(bf16)

    lane = iota((16, 192), 1)
    sub = iota((16, 192), 0)
    seg = lane & 63
    part = seg >> 4
    step = row_of_place(seg & 15) - (sub & 7)
    tap_masks = []
    for i in range(3):
        for j in range(3):
            tap_masks.append((part == j) & (step == 2 * (i - 1)))
    bias_mask = seg == 48
    first = sub < 8

    def paint_pair(c, carry):
        value = jnp.where(bias_mask, jnp.where(first, bias[2 * c], bias[2 * c + 1]), 0.0)
        for tap in range(9):
            pair = jnp.where(first, weight[tap, 2 * c], weight[tap, 2 * c + 1])
            value = jnp.where(tap_masks[tap], pair, value)
        paint_lhs[pl.ds(pl.multiple_of(c * 16, 16), 16), :] = pack(value, lane, 64)
        return carry

    lax.fori_loop(0, channels // 2, paint_pair, 0)
    one_row = jnp.where(iota((16, block), 0) == 0, 1.0, 0.0).astype(f32)

    lane = iota((16, 240), 1)
    sub = iota((16, 240), 0)
    seg = jnp.where(lane >= 160, lane - 160, jnp.where(lane >= 80, lane - 80, lane))
    part = seg >> 4
    step = row_of_place(seg & 15) - jnp.where(sub < 8, sub, jnp.where(sub == 8, -1, 8))
    value = jnp.zeros((16, 240), f32)
    for a in range(5):
        for b in range(5):
            value = jnp.where((part == b) & (step == a - 2) & (sub < 10), short[a, b], value)
    short_lhs[...] = pack(value, lane, 80)

    spread[...] = ((iota((128, block), 1) >> 2) == iota((128, block), 0)).astype(f32).astype(bf16)
    pool = ((iota((block, 128), 0) >> 2) == iota((block, 128), 1)).astype(f32).astype(bf16)
    col_scale = cols / 16.0

    def col_rows(i, carry):
        gap = iota((64, coarse_cols), 0) + i * 64 - iota((64, coarse_cols), 1)
        hi, lo = split(jnp.exp(-jnp.abs(gap.astype(f32)) / col_scale))
        at = pl.ds(pl.multiple_of(i * 64, 64), 64)
        col_hi[at, :] = hi
        col_lo[at, :] = lo
        return carry

    lax.fori_loop(0, coarse_cols // 64, col_rows, 0)
    own_copy.wait()
    edge_wait(mass_copy, 0)

    def paint(cb):
        sums = []
        for p in range(planes):
            parts = [mass_edge[p, :, at_window(cb)], mass_own[p, :, at_window(cb)]]
            stacked = []
            for j in range(3):
                start = pad + 2 * (j - 1)
                stacked += [x[:, start : start + block] for x in parts]
            stacked.append(one_row)
            hi, lo = split(jnp.concatenate(stacked, axis=0))
            pre = dot(paint_lhs[...], jnp.concatenate([hi, lo, hi], axis=0))
            total = jnp.zeros((rows, block), f32)
            for c in range(channels):
                total += mix[c] * jnp.tanh(pre[rows * c : rows * c + rows])
            conv_own[p, :, at_padded(cb)] = total
            sums.append(jnp.sum(total[0:4], axis=0, keepdims=True))
            sums.append(jnp.sum(total[4:8], axis=0, keepdims=True))
        sums += [jnp.zeros((1, block), f32)] * (8 - 2 * planes)
        hi, lo = split(jnp.concatenate(sums, axis=0) * (1.0 / 16.0))
        coarse = dot(hi, pool) + dot(lo, pool)
        gathered[t, :, pl.ds(pl.multiple_of(cb * 128, 128), 128)] = coarse

    def short_copy(cb, to):
        return pltpu.make_async_remote_copy(
            src_ref=shorts.at[g, :, :, at_padded(cb)],
            dst_ref=shorts.at[g, :, :, at_padded(cb)],
            send_sem=short_send.at[to, cb],
            recv_sem=short_recv.at[g, cb],
            device_id={"plane": to},
        )

    def long_copy(to):
        return pltpu.make_async_remote_copy(
            src_ref=longs.at[g],
            dst_ref=longs.at[g],
            send_sem=long_send.at[to],
            recv_sem=long_recv.at[g],
            device_id={"plane": to},
        )

    def short_block(cb):
        edges = []
        for p in range(planes):
            parts = [conv_edge[p, :, at_window(cb)], conv_own[p, :, at_window(cb)]]
            stacked = [
                x[:, pad + b - 2 : pad + b - 2 + block] for b in range(5) for x in parts
            ]
            hi, lo = split(jnp.concatenate(stacked, axis=0))
            value = dot(short_lhs[...], jnp.concatenate([hi, lo, hi], axis=0))
            shorts[g, p, :, at_padded(cb)] = value[0:8]
            edges.append(value[8:10])
        edges += [jnp.zeros((8 - 2 * planes, block), f32)]
        shorts[g, planes, :, at_padded(cb)] = jnp.concatenate(edges, axis=0)

        def short_start(to, carry):
            short_copy(cb, to).start()
            return carry

        lax.fori_loop(g + 1, groups, short_start, 0)

    def coarse_copy(j):
        return pltpu.make_async_remote_copy(
            src_ref=gathered.at[t],
            dst_ref=gathered.at[t],
            send_sem=coarse_send.at[j],
            recv_sem=coarse_recv.at[t],
            device_id={"tile": lax.rem(t + j, tiles)},
        )

    def coarse_start(j, carry):
        coarse_copy(j).start()
        return carry

    def paint_step(cb, carry):
        @pl.when(cb + 1 < blocks)
        def _():
            edge_wait(mass_copy, cb + 1)

        paint(cb)

        @pl.when(cb + 1 < blocks)
        def _():
            edge_start(conv_copy, cb)

        @pl.when(cb == 2)
        def _():
            edge_wait(conv_copy, 0)

        @pl.when(cb > 1)
        def _():
            edge_wait(conv_copy, cb - 1)
            short_block(cb - 2)

        return carry

    lax.fori_loop(0, blocks, paint_step, 0)
    lax.fori_loop(1, tiles, coarse_start, 0)
    edge_start(conv_copy, blocks - 1)
    short_rest = max(blocks - 2, 0)

    def short_step(cb, carry):
        @pl.when(cb + 1 < blocks)
        def _():
            edge_wait(conv_copy, cb + 1)

        short_block(cb)
        return carry

    lax.fori_loop(short_rest, blocks, short_step, 0)

    def coarse_wait(j, carry):
        source = lax.rem(t + j, tiles)
        pltpu.make_async_remote_copy(
            src_ref=gathered.at[source],
            dst_ref=gathered.at[source],
            send_sem=coarse_send.at[j],
            recv_sem=coarse_recv.at[source],
            device_id={"tile": source},
        ).wait_recv()
        return carry

    row_scale = tiles * rows / 16.0
    long_gain = 1.0 / math.sqrt(row_scale * col_scale)
    m = iota((16, tiles * 8), 0)
    n = iota((16, tiles * 8), 1)
    gap = (2 * t - 1 + (m & 3)) - (2 * (n >> 3) + (n & 1))
    near = jnp.exp(-jnp.abs(gap.astype(f32)) / row_scale) * long_gain
    row_kernel = jnp.where((m >> 2) == ((n & 7) >> 1), near, 0.0)
    row_hi, row_lo = split(row_kernel)
    row_lhs = jnp.concatenate([row_hi, row_hi, row_lo], axis=1)
    lax.fori_loop(1, tiles, coarse_wait, 0)
    hi, lo = split(gathered[...].reshape(tiles * 8, coarse_cols))
    hi, lo = split(dot(row_lhs, jnp.concatenate([hi, lo, hi], axis=0)))
    both = dot(jnp.concatenate([hi, lo], axis=0), col_hi[...])
    longs[g] = both[0:16] + both[16:32] + dot(hi, col_lo[...])

    def long_start(to, carry):
        long_copy(to).start()
        return carry

    lax.fori_loop(g + 1, groups, long_start, 0)

    for entry in range(4):
        for p in (planes - 2, planes - 1):
            state[entry, p] = jnp.full((rows, cols), 1.0 if entry in (0, 3) else 0.0, f32)
    row_at = iota((rows, block + 2 * pad), 0)
    low_gain = jnp.where(t > 0, 1.0, 0.0)
    high_gain = jnp.where(t < tiles - 1, 1.0, 0.0)
    slot_total = 2.0 * slots
    pieces = coarse_cols // 128

    def out_copy(cb):
        return pltpu.make_async_copy(
            state.at[:, :, :, at_block(cb)], out.at[:, :, :, at_block(cb)], out_sem.at[cb]
        )

    def lens(gi, carry):
        @pl.when(gi < g)
        def _():
            def short_wait(cb, inner):
                pltpu.make_async_remote_copy(
                    src_ref=shorts.at[gi, :, :, at_padded(cb)],
                    dst_ref=shorts.at[gi, :, :, at_padded(cb)],
                    send_sem=short_send.at[gi, cb],
                    recv_sem=short_recv.at[gi, cb],
                    device_id={"plane": gi},
                ).wait_recv()
                return inner

            lax.fori_loop(0, blocks, short_wait, 0)
            pltpu.make_async_remote_copy(
                src_ref=longs.at[gi],
                dst_ref=longs.at[gi],
                send_sem=long_send.at[gi],
                recv_sem=long_recv.at[gi],
                device_id={"plane": gi},
            ).wait_recv()

        hi, lo = split(longs[gi])
        stacked = [x[:, 128 * b : 128 * b + 128] for x in (hi, lo) for b in range(pieces)]
        spread_out = dot(jnp.concatenate(stacked, axis=0), spread[...])
        for b in range(pieces):
            long_wide[:, pad + b * block : pad + b * block + block] = (
                spread_out[16 * b : 16 * b + 16]
                + spread_out[16 * (pieces + b) : 16 * (pieces + b) + 16]
            )

        factors = []
        for p in range(planes):
            k = gi * planes + p

            def distance(index):
                value = jnp.full((8, 128), slot[index], jnp.int32)
                return (value.astype(f32) + 1.0) / slot_total

            here = distance(k)
            before = jnp.where(k > 0, distance(jnp.maximum(k - 1, 0)), 0.0)
            after = jnp.where(
                k < slots - 1,
                distance(jnp.minimum(k + 1, slots - 1)),
                (slot_total + 1.0) / slot_total,
            )
            mixing = before * (after - here) / (here * (after - before))
            bending = lens_gain * (after - here) / after
            factors.append((mixing, bending))

        def lens_block(cb, inner):
            at = at_block(cb)
            edges = shorts[gi, planes, :, at_window(cb)]
            longer = long_wide[:, at_window(cb)]
            old = [state[e, planes - 2, :, at] for e in range(4)]
            new = [state[e, planes - 1, :, at] for e in range(4)]
            for p in range(planes):
                mixing, bending = [
                    jnp.concatenate([x] * (block // 128), axis=1) for x in factors[p]
                ]
                center = shorts[gi, p, :, at_window(cb)] + jnp.where(
                    row_at < 4, longer[4 * p + 1 : 4 * p + 2], longer[4 * p + 2 : 4 * p + 3]
                )
                top = (edges[2 * p : 2 * p + 1] + longer[4 * p : 4 * p + 1]) * low_gain
                bottom = (
                    edges[2 * p + 1 : 2 * p + 2] + longer[4 * p + 3 : 4 * p + 4]
                ) * high_gain
                up = jnp.where(row_at == 0, top, pltpu.roll(center, 1, 0))
                down = jnp.where(row_at == rows - 1, bottom, pltpu.roll(center, rows - 1, 0))

                def moved(x, by):
                    return x[:, pad + by : pad + by + block]

                here = moved(center, 0) * 2.0
                slope = down - up
                u11 = (moved(down, 0) + moved(up, 0) - here) * bending
                u22 = (moved(center, 1) + moved(center, -1) - here) * bending
                u12 = (moved(slope, 1) - moved(slope, -1)) * (0.25 * bending)
                bent = [
                    u11 * new[0] + u12 * new[2],
                    u11 * new[1] + u12 * new[3],
                    u12 * new[0] + u22 * new[2],
                    u12 * new[1] + u22 * new[3],
                ]
                keep = 1.0 - mixing
                advanced = [keep * old[e] + mixing * new[e] - bent[e] for e in range(4)]
                for e in range(4):
                    state[e, p, :, at] = advanced[e]
                old, new = new, advanced

            @pl.when(gi == g)
            def _():
                out_copy(cb).start()

            return inner

        lax.fori_loop(0, blocks, lens_block, 0)
        return carry

    lax.fori_loop(0, g + 1, lens, 0)

    def block_sent(cb, carry):
        edge_sent(mass_copy, cb)
        edge_sent(conv_copy, cb)
        return carry

    lax.fori_loop(0, blocks, block_sent, 0)

    def coarse_sent(j, carry):
        coarse_copy(j).wait_send()
        return carry

    lax.fori_loop(1, tiles, coarse_sent, 0)

    def later_sent(to, carry):
        def short_sent(cb, inner):
            short_copy(cb, to).wait_send()
            return inner

        lax.fori_loop(0, blocks, short_sent, 0)
        long_copy(to).wait_send()
        return carry

    lax.fori_loop(g + 1, groups, later_sent, 0)

    def out_done(cb, carry):
        out_copy(cb).wait()
        return carry

    lax.fori_loop(0, blocks, out_done, 0)


def solution(mesh):
    tiles, groups = mesh.shape["tile"], mesh.shape["plane"]

    def body(density, plane_slot, paint_weight, paint_bias, mix_weight, short_kernel):
        planes, rows, cols = density.shape
        channels = paint_weight.shape[0]
        coarse_cols = cols // 4
        blocks = cols // block
        place = pl.BlockSpec(memory_space=pltpu.HBM)
        smem = pl.BlockSpec(memory_space=pltpu.SMEM)
        wide = cols + 2 * pad
        dma = pltpu.SemaphoreType.DMA
        map_shape = pltpu.VMEM((planes, rows, wide), f32)
        return pl.pallas_call(
            functools.partial(kernel, tiles, groups),
            out_shape=jax.ShapeDtypeStruct((4, planes, rows, cols), f32),
            in_specs=[place] + [smem] * 5,
            out_specs=place,
            scratch_shapes=[
                map_shape,
                map_shape,
                map_shape,
                map_shape,
                pltpu.VMEM((8 * channels, 192), bf16),
                pltpu.VMEM((16, 240), bf16),
                pltpu.VMEM((coarse_cols, coarse_cols), bf16),
                pltpu.VMEM((coarse_cols, coarse_cols), bf16),
                pltpu.VMEM((128, block), bf16),
                pltpu.VMEM((tiles, 8, coarse_cols), f32),
                pltpu.VMEM((groups, planes + 1, rows, wide), f32),
                pltpu.VMEM((groups, 16, coarse_cols), f32),
                pltpu.VMEM((16, wide), f32),
                pltpu.VMEM((4, planes, rows, cols), f32),
                dma(()),
                dma((blocks,)),
                dma((2, blocks)),
                dma((2, blocks)),
                dma((2, blocks)),
                dma((2, blocks)),
                dma((tiles,)),
                dma((tiles,)),
                dma((groups, blocks)),
                dma((groups, blocks)),
                dma((groups,)),
                dma((groups,)),
            ],
            compiler_params=pltpu.CompilerParams(
                collective_id=0, has_side_effects=True, vmem_limit_bytes=60 * 1024 * 1024
            ),
        )(density, plane_slot, paint_weight.T, paint_bias, mix_weight, short_kernel)

    placed = (P("plane", "tile", None), P(), P(), P(), P(), P())
    return jax.shard_map(
        body, mesh=mesh, in_specs=placed, out_specs=P(None, "plane", "tile", None), check_vma=False
    )
```

time: 31.8 us -> 38 us (1.19)
  Pallas kernels: 27.7 us -> 35.7 us
  local copies, waits for them, and re-layouts: 3.87 us -> 2.06 us
    pallas_call x1, Pallas kernels: 27.7 us -> 35.7 us  [body(): pl.pallas_call(functools.partial(kernel, tiles, groups), out_shape=jax.Sh...]
    unnamed x13 -> x1, local copies, waits for them, and re-layouts: 3.87 us -> 2.06 us
where the time goes in v3:
time: 38 us; the launch traced here: 37.8 us
  Pallas kernels  35.7 us (94%)
  local copies, waits for them, and re-layouts  2.06 us (5%)
    pallas_call x1, Pallas kernels, body(): pl.pallas_call(functools.partial(kernel, tiles, groups), out_shape=jax.Sh...  35.7 us
    unnamed x1, local copies, waits for them, and re-layouts  2.06 us

profile of v3, /device:TPU:15, one launch (start us, length us, event | category | flops | bytes accessed | tf_op | source)
XLA Modules:
  0.0 37.8 jit_solution(7275751826604152797)
XLA Ops:
  0.0 35.7 %shard_map.64 = f32[4,3,8,2048]{3,2,1,0:T(8,128)} custom-call(f32[3,8,2048]{2,1,0:T(8,128)} %density.1, s32[12]{0:T(128)} %slot.1, f32[9,32]{1,0:T(8,128)} %bitcast.1, f32[32]{0:T(128)} %bias.1, f32[32]{0:T(128)} %mix.1, f32[5,5]{1,0:T(8,128)} %short.1), custom_call_target="tpu_custom_call" | custom-call | tf_op jit(solution)/shard_map/pallas_call | solution.py:501
  35.7 2.1 %copy.8 = f32[4,3,8,2048]{3,2,1,0:T(8,128)} copy(f32[4,3,8,2048]{3,2,1,0:T(8,128)} %shard_map.64) | data formatting | bytes 1572864

commit v4 on v3

--- a/solution.py
+++ b/solution.py
@@ -31,14 +31,14 @@
 def kernel(
     tiles, groups, density, slot, weight, bias, mix, short, out,
     mass_own, mass_edge, conv_own, conv_edge, paint_lhs, short_lhs, col_hi, col_lo, spread,
-    gathered, shorts, longs, long_wide, state,
-    own_sem, out_sem, mass_send, mass_recv, conv_send, conv_recv, coarse_send, coarse_recv,
+    gathered, shorts, longs,
+    mass_send, mass_recv, conv_send, conv_recv, coarse_send, coarse_recv,
     short_send, short_recv, long_send, long_recv,
 ):
     planes, rows, cols = density.shape
-    channels = weight.shape[1]
+    channels = weight.shape[0]
+    slots = slot.shape[0]
     blocks = cols // block
-    slots = slot.shape[0]
     coarse_cols = cols // 4
     half = rows // 2
     t = lax.axis_index("tile")
@@ -55,8 +55,9 @@
     def at_window(cb):
         return pl.ds(pl.multiple_of(cb * block, block), block + 2 * pad)
 
-    own_copy = pltpu.make_async_copy(density, mass_own.at[:, :, pl.ds(pad, cols)], own_sem)
-    own_copy.start()
+    def shifted(x, by):
+        moved = x if by == 0 else pltpu.roll(x, (-by) % (block + 2 * pad), 1)
+        return moved[:, pad : pad + block]
 
     barrier = pltpu.get_barrier_semaphore()
 
@@ -134,11 +135,6 @@
         @pl.when(jnp.logical_not(has_high))
         def _():
             buffer[:, half:rows, pad : pad + cols] = jnp.zeros((planes, half, cols), f32)
-
-    shorts[:, :, :, 0:pad] = jnp.zeros((groups, planes + 1, rows, pad), f32)
-    shorts[:, :, :, pad + cols :] = jnp.zeros((groups, planes + 1, rows, pad), f32)
-    long_wide[:, 0:pad] = jnp.zeros((16, pad), f32)
-    long_wide[:, pad + cols :] = jnp.zeros((16, pad), f32)
 
     def row_of_place(place):
         return jnp.where(place < half, place - half, jnp.where(place < rows, place + half, place - rows))
@@ -162,7 +158,7 @@
     def paint_pair(c, carry):
         value = jnp.where(bias_mask, jnp.where(first, bias[2 * c], bias[2 * c + 1]), 0.0)
         for tap in range(9):
-            pair = jnp.where(first, weight[tap, 2 * c], weight[tap, 2 * c + 1])
+            pair = jnp.where(first, weight[2 * c, tap], weight[2 * c + 1, tap])
             value = jnp.where(tap_masks[tap], pair, value)
         paint_lhs[pl.ds(pl.multiple_of(c * 16, 16), 16), :] = pack(value, lane, 64)
         return carry
@@ -194,7 +190,7 @@
         return carry
 
     lax.fori_loop(0, coarse_cols // 64, col_rows, 0)
-    own_copy.wait()
+    mass_own[:, :, pad : pad + cols] = density[...]
     edge_wait(mass_copy, 0)
 
     def paint(cb):
@@ -203,8 +199,7 @@
             parts = [mass_edge[p, :, at_window(cb)], mass_own[p, :, at_window(cb)]]
             stacked = []
             for j in range(3):
-                start = pad + 2 * (j - 1)
-                stacked += [x[:, start : start + block] for x in parts]
+                stacked += [shifted(x, 2 * (j - 1)) for x in parts]
             stacked.append(one_row)
             hi, lo = split(jnp.concatenate(stacked, axis=0))
             pre = dot(paint_lhs[...], jnp.concatenate([hi, lo, hi], axis=0))
@@ -221,8 +216,8 @@
 
     def short_copy(cb, to):
         return pltpu.make_async_remote_copy(
-            src_ref=shorts.at[g, :, :, at_padded(cb)],
-            dst_ref=shorts.at[g, :, :, at_padded(cb)],
+            src_ref=shorts.at[g, :, :, at_block(cb)],
+            dst_ref=shorts.at[g, :, :, at_block(cb)],
             send_sem=short_send.at[to, cb],
             recv_sem=short_recv.at[g, cb],
             device_id={"plane": to},
@@ -241,15 +236,13 @@
         edges = []
         for p in range(planes):
             parts = [conv_edge[p, :, at_window(cb)], conv_own[p, :, at_window(cb)]]
-            stacked = [
-                x[:, pad + b - 2 : pad + b - 2 + block] for b in range(5) for x in parts
-            ]
+            stacked = [shifted(x, b - 2) for b in range(5) for x in parts]
             hi, lo = split(jnp.concatenate(stacked, axis=0))
             value = dot(short_lhs[...], jnp.concatenate([hi, lo, hi], axis=0))
-            shorts[g, p, :, at_padded(cb)] = value[0:8]
+            shorts[g, p, :, at_block(cb)] = value[0:8]
             edges.append(value[8:10])
         edges += [jnp.zeros((8 - 2 * planes, block), f32)]
-        shorts[g, planes, :, at_padded(cb)] = jnp.concatenate(edges, axis=0)
+        shorts[g, planes, :, at_block(cb)] = jnp.concatenate(edges, axis=0)
 
         def short_start(to, carry):
             short_copy(cb, to).start()
@@ -341,30 +334,33 @@
 
     for entry in range(4):
         for p in (planes - 2, planes - 1):
-            state[entry, p] = jnp.full((rows, cols), 1.0 if entry in (0, 3) else 0.0, f32)
-    row_at = iota((rows, block + 2 * pad), 0)
+            out[entry, p] = jnp.full((rows, cols), 1.0 if entry in (0, 3) else 0.0, f32)
+    row_at = iota((rows, cols), 0)
+    col_at = iota((rows, cols), 1)
     low_gain = jnp.where(t > 0, 1.0, 0.0)
     high_gain = jnp.where(t < tiles - 1, 1.0, 0.0)
     slot_total = 2.0 * slots
-    pieces = coarse_cols // 128
-
-    def out_copy(cb):
-        return pltpu.make_async_copy(
-            state.at[:, :, :, at_block(cb)], out.at[:, :, :, at_block(cb)], out_sem.at[cb]
-        )
+    wide = cols // 128
+
+    def next_col(x):
+        return jnp.where(col_at == cols - 1, 0.0, pltpu.roll(x, cols - 1, 1))
+
+    def last_col(x):
+        return jnp.where(col_at == 0, 0.0, pltpu.roll(x, 1, 1))
 
     def lens(gi, carry):
         @pl.when(gi < g)
         def _():
-            def short_wait(cb, inner):
+            def short_wait(cb, carry):
+                at = pl.ds(pl.multiple_of(cb * block, block), block)
                 pltpu.make_async_remote_copy(
-                    src_ref=shorts.at[gi, :, :, at_padded(cb)],
-                    dst_ref=shorts.at[gi, :, :, at_padded(cb)],
+                    src_ref=shorts.at[gi, :, :, at],
+                    dst_ref=shorts.at[gi, :, :, at],
                     send_sem=short_send.at[gi, cb],
                     recv_sem=short_recv.at[gi, cb],
                     device_id={"plane": gi},
                 ).wait_recv()
-                return inner
+                return carry
 
             lax.fori_loop(0, blocks, short_wait, 0)
             pltpu.make_async_remote_copy(
@@ -376,15 +372,16 @@
             ).wait_recv()
 
         hi, lo = split(longs[gi])
+        pieces = coarse_cols // 128
         stacked = [x[:, 128 * b : 128 * b + 128] for x in (hi, lo) for b in range(pieces)]
         spread_out = dot(jnp.concatenate(stacked, axis=0), spread[...])
-        for b in range(pieces):
-            long_wide[:, pad + b * block : pad + b * block + block] = (
-                spread_out[16 * b : 16 * b + 16]
-                + spread_out[16 * (pieces + b) : 16 * (pieces + b) + 16]
-            )
-
-        factors = []
+        upper = [
+            spread_out[16 * b : 16 * b + 16]
+            + spread_out[16 * (pieces + b) : 16 * (pieces + b) + 16]
+            for b in range(pieces)
+        ]
+        long_wide = jnp.concatenate(upper, axis=1)
+        edges = shorts[gi, planes]
         for p in range(planes):
             k = gi * planes + p
 
@@ -401,55 +398,31 @@
             )
             mixing = before * (after - here) / (here * (after - before))
             bending = lens_gain * (after - here) / after
-            factors.append((mixing, bending))
-
-        def lens_block(cb, inner):
-            at = at_block(cb)
-            edges = shorts[gi, planes, :, at_window(cb)]
-            longer = long_wide[:, at_window(cb)]
-            old = [state[e, planes - 2, :, at] for e in range(4)]
-            new = [state[e, planes - 1, :, at] for e in range(4)]
-            for p in range(planes):
-                mixing, bending = [
-                    jnp.concatenate([x] * (block // 128), axis=1) for x in factors[p]
-                ]
-                center = shorts[gi, p, :, at_window(cb)] + jnp.where(
-                    row_at < 4, longer[4 * p + 1 : 4 * p + 2], longer[4 * p + 2 : 4 * p + 3]
-                )
-                top = (edges[2 * p : 2 * p + 1] + longer[4 * p : 4 * p + 1]) * low_gain
-                bottom = (
-                    edges[2 * p + 1 : 2 * p + 2] + longer[4 * p + 3 : 4 * p + 4]
-                ) * high_gain
-                up = jnp.where(row_at == 0, top, pltpu.roll(center, 1, 0))
-                down = jnp.where(row_at == rows - 1, bottom, pltpu.roll(center, rows - 1, 0))
-
-                def moved(x, by):
-                    return x[:, pad + by : pad + by + block]
-
-                here = moved(center, 0) * 2.0
-                slope = down - up
-                u11 = (moved(down, 0) + moved(up, 0) - here) * bending
-                u22 = (moved(center, 1) + moved(center, -1) - here) * bending
-                u12 = (moved(slope, 1) - moved(slope, -1)) * (0.25 * bending)
-                bent = [
-                    u11 * new[0] + u12 * new[2],
-                    u11 * new[1] + u12 * new[3],
-                    u12 * new[0] + u22 * new[2],
-                    u12 * new[1] + u22 * new[3],
-                ]
-                keep = 1.0 - mixing
-                advanced = [keep * old[e] + mixing * new[e] - bent[e] for e in range(4)]
-                for e in range(4):
-                    state[e, p, :, at] = advanced[e]
-                old, new = new, advanced
-
-            @pl.when(gi == g)
-            def _():
-                out_copy(cb).start()
-
-            return inner
-
-        lax.fori_loop(0, blocks, lens_block, 0)
+            mixing = jnp.concatenate([mixing] * wide, axis=1)
+            bending = jnp.concatenate([bending] * wide, axis=1)
+            center = shorts[gi, p] + jnp.where(
+                row_at < 4, long_wide[4 * p + 1 : 4 * p + 2], long_wide[4 * p + 2 : 4 * p + 3]
+            )
+            top = (edges[2 * p : 2 * p + 1] + long_wide[4 * p : 4 * p + 1]) * low_gain
+            bottom = (
+                edges[2 * p + 1 : 2 * p + 2] + long_wide[4 * p + 3 : 4 * p + 4]
+            ) * high_gain
+            up = jnp.where(row_at == 0, top, pltpu.roll(center, 1, 0))
+            down = jnp.where(row_at == rows - 1, bottom, pltpu.roll(center, rows - 1, 0))
+            u11 = (down - 2.0 * center + up) * bending
+            u22 = (next_col(center) - 2.0 * center + last_col(center)) * bending
+            slope = down - up
+            u12 = (next_col(slope) - last_col(slope)) * (0.25 * bending)
+            old = [out[e, (p - 2) % planes] for e in range(4)]
+            new = [out[e, (p - 1) % planes] for e in range(4)]
+            bent = [
+                u11 * new[0] + u12 * new[2],
+                u11 * new[1] + u12 * new[3],
+                u12 * new[0] + u22 * new[2],
+                u12 * new[1] + u22 * new[3],
+            ]
+            for e in range(4):
+                out[e, p] = (1.0 - mixing) * old[e] + mixing * new[e] - bent[e]
         return carry
 
     lax.fori_loop(0, g + 1, lens, 0)
@@ -477,12 +450,6 @@
         return carry
 
     lax.fori_loop(g + 1, groups, later_sent, 0)
-
-    def out_done(cb, carry):
-        out_copy(cb).wait()
-        return carry
-
-    lax.fori_loop(0, blocks, out_done, 0)
 
 
 def solution(mesh):
@@ -493,7 +460,7 @@
         channels = paint_weight.shape[0]
         coarse_cols = cols // 4
         blocks = cols // block
-        place = pl.BlockSpec(memory_space=pltpu.HBM)
+        vmem = pl.BlockSpec(memory_space=pltpu.VMEM)
         smem = pl.BlockSpec(memory_space=pltpu.SMEM)
         wide = cols + 2 * pad
         dma = pltpu.SemaphoreType.DMA
@@ -501,8 +468,8 @@
         return pl.pallas_call(
             functools.partial(kernel, tiles, groups),
             out_shape=jax.ShapeDtypeStruct((4, planes, rows, cols), f32),
-            in_specs=[place] + [smem] * 5,
-            out_specs=place,
+            in_specs=[vmem] + [smem] * 5,
+            out_specs=vmem,
             scratch_shapes=[
                 map_shape,
                 map_shape,
@@ -514,12 +481,8 @@
                 pltpu.VMEM((coarse_cols, coarse_cols), bf16),
                 pltpu.VMEM((128, block), bf16),
                 pltpu.VMEM((tiles, 8, coarse_cols), f32),
-                pltpu.VMEM((groups, planes + 1, rows, wide), f32),
+                pltpu.VMEM((groups, planes + 1, rows, cols), f32),
                 pltpu.VMEM((groups, 16, coarse_cols), f32),
-                pltpu.VMEM((16, wide), f32),
-                pltpu.VMEM((4, planes, rows, cols), f32),
-                dma(()),
-                dma((blocks,)),
                 dma((2, blocks)),
                 dma((2, blocks)),
                 dma((2, blocks)),
@@ -532,9 +495,9 @@
                 dma((groups,)),
             ],
             compiler_params=pltpu.CompilerParams(
-                collective_id=0, has_side_effects=True, vmem_limit_bytes=60 * 1024 * 1024
+                collective_id=0, has_side_effects=True, vmem_limit_bytes=48 * 1024 * 1024
             ),
-        )(density, plane_slot, paint_weight.T, paint_bias, mix_weight, short_kernel)
+        )(density, plane_slot, paint_weight, paint_bias, mix_weight, short_kernel)
 
     placed = (P("plane", "tile", None), P(), P(), P(), P(), P())
     return jax.shard_map(

time: 38 us -> 30.4 us (0.80)
  Pallas kernels: 35.7 us -> 27.5 us
  local copies, waits for them, and re-layouts: 2.06 us -> 2.64 us
    pallas_call x1, Pallas kernels: 35.7 us -> 27.5 us  [body(): pl.pallas_call(functools.partial(kernel, tiles, groups), out_shape=jax.Sh...]
    unnamed x1 -> x12, local copies, waits for them, and re-layouts: 2.06 us -> 2.64 us
where the time goes in v4:
time: 30.4 us; the launch traced here: 30.2 us
  Pallas kernels  27.5 us (90%)
  local copies, waits for them, and re-layouts  2.64 us (9%)
    pallas_call x1, Pallas kernels, body(): pl.pallas_call(functools.partial(kernel, tiles, groups), out_shape=jax.Sh...  27.5 us
    unnamed x12, local copies, waits for them, and re-layouts  2.64 us

profile of v4, /device:TPU:15, one launch (start us, length us, event | category | flops | bytes accessed | tf_op | source)
XLA Modules:
  0.0 30.2 jit_solution(12698896290909081165)
XLA Ops:
  0.0 0.0 copy-start.1
  0.0 0.0 copy-start.4
  0.0 0.0 copy-start.3
  0.0 0.0 copy-start.2
  0.0 0.8 %copy.7.weight = f32[32,9]{1,0:T(8,128)S(1)} copy(f32[32,9]{0,1:T(8,128)} %param.8) | data formatting | bytes 2304 | tf_op args[2]
  0.8 0.0 copy-done.1
  0.8 0.0 copy-done.4
  0.8 0.0 copy-done.3
  0.9 0.0 copy-done.2
  0.9 0.0 copy-start
  0.9 0.9 %copy-done = f32[3,8,2048]{2,1,0:T(8,128)S(1)} copy-done((f32[3,8,2048]{2,1,0:T(8,128)S(1)}, f32[3,8,2048]{2,1,0:T(8,128)}, u32[]{:S(2)}) %copy-start) | copy-done | bytes 196632
  1.8 27.5 %shard_map.64 = f32[4,3,8,2048]{3,2,1,0:T(8,128)S(1)} custom-call(f32[3,8,2048]{2,1,0:T(8,128)S(1)} %copy-done, s32[12]{0:T(128)S(1)} %copy-done.2, f32[32,9]{1,0:T(8,128)S(1)} %copy.7.weight, f32[32]{0:T(128)S(1)} %copy-done.3, f32[32]{0:T(128)S(1)} %copy-done.4, f32[5,5]{1,0:T(8,128)S(1)} %copy-done.1), custom_call_target="tpu_custom_call" | custom-call | tf_op jit(solution)/shard_map/pallas_call | solution.py:468
  29.3 0.9 %copy.9 = f32[4,3,8,2048]{3,2,1,0:T(8,128)} copy(f32[4,3,8,2048]{3,2,1,0:T(8,128)S(1)} %shard_map.64) | data formatting | bytes 1572864
Async XLA Ops:
  0.0 0.8 %copy-start.1 = (f32[5,5]{1,0:T(8,128)S(1)}, f32[5,5]{1,0:T(8,128)}, u32[]{:S(2)}) copy-start(f32[5,5]{1,0:T(8,128)} %short.1) | copy-start | bytes 304
  0.0 0.8 %copy-start.4 = (f32[32]{0:T(128)S(1)}, f32[32]{0:T(128)}, u32[]{:S(2)}) copy-start(f32[32]{0:T(128)} %mix.1) | copy-start | bytes 388
  0.0 0.8 %copy-start.3 = (f32[32]{0:T(128)S(1)}, f32[32]{0:T(128)}, u32[]{:S(2)}) copy-start(f32[32]{0:T(128)} %bias.1) | copy-start | bytes 388
  0.0 0.8 %copy-start.2 = (s32[12]{0:T(128)S(1)}, s32[12]{0:T(128)}, u32[]{:S(2)}) copy-start(s32[12]{0:T(128)} %slot.1) | copy-start | bytes 148
  0.9 0.9 %copy-start = (f32[3,8,2048]{2,1,0:T(8,128)S(1)}, f32[3,8,2048]{2,1,0:T(8,128)}, u32[]{:S(2)}) copy-start(f32[3,8,2048]{2,1,0:T(8,128)} %density.1) | copy-start | bytes 589828

commit v5 on v4

--- a/solution.py
+++ b/solution.py
@@ -10,7 +10,8 @@
 
 lens_gain = 0.25
 pad = 128
-block = 512
+block = 256
+span = 512
 f32 = jnp.float32
 bf16 = jnp.bfloat16
 
@@ -31,7 +32,7 @@
 def kernel(
     tiles, groups, density, slot, weight, bias, mix, short, out,
     mass_own, mass_edge, conv_own, conv_edge, paint_lhs, short_lhs, col_hi, col_lo, spread,
-    gathered, shorts, longs,
+    gathered, shorts, longs, row_sums, field_own, field_now,
     mass_send, mass_recv, conv_send, conv_recv, coarse_send, coarse_recv,
     short_send, short_recv, long_send, long_recv,
 ):
@@ -177,8 +178,8 @@
             value = jnp.where((part == b) & (step == a - 2) & (sub < 10), short[a, b], value)
     short_lhs[...] = pack(value, lane, 80)
 
-    spread[...] = ((iota((128, block), 1) >> 2) == iota((128, block), 0)).astype(f32).astype(bf16)
-    pool = ((iota((block, 128), 0) >> 2) == iota((block, 128), 1)).astype(f32).astype(bf16)
+    spread[...] = ((iota((128, span), 1) >> 2) == iota((128, span), 0)).astype(f32).astype(bf16)
+    pool = ((iota((span, 128), 0) >> 2) == iota((span, 128), 1)).astype(f32).astype(bf16)
     col_scale = cols / 16.0
 
     def col_rows(i, carry):
@@ -210,9 +211,18 @@
             sums.append(jnp.sum(total[0:4], axis=0, keepdims=True))
             sums.append(jnp.sum(total[4:8], axis=0, keepdims=True))
         sums += [jnp.zeros((1, block), f32)] * (8 - 2 * planes)
-        hi, lo = split(jnp.concatenate(sums, axis=0) * (1.0 / 16.0))
-        coarse = dot(hi, pool) + dot(lo, pool)
-        gathered[t, :, pl.ds(pl.multiple_of(cb * 128, 128), 128)] = coarse
+        row_sums[:, at_block(cb)] = jnp.concatenate(sums, axis=0) * (1.0 / 16.0)
+
+    def pool_columns():
+        count = cols // span
+        sums = row_sums[...]
+        pieces = [sums[:, span * b : span * b + span] for b in range(count)]
+        hi, lo = split(jnp.concatenate(pieces, axis=0))
+        pooled = dot(jnp.concatenate([hi, lo], axis=0), pool)
+        for b in range(count):
+            gathered[t, :, 128 * b : 128 * b + 128] = (
+                pooled[8 * b : 8 * b + 8] + pooled[8 * (count + b) : 8 * (count + b) + 8]
+            )
 
     def short_copy(cb, to):
         return pltpu.make_async_remote_copy(
@@ -286,6 +296,7 @@
         return carry
 
     lax.fori_loop(0, blocks, paint_step, 0)
+    pool_columns()
     lax.fori_loop(1, tiles, coarse_start, 0)
     edge_start(conv_copy, blocks - 1)
     short_rest = max(blocks - 2, 0)
@@ -348,29 +359,7 @@
     def last_col(x):
         return jnp.where(col_at == 0, 0.0, pltpu.roll(x, 1, 1))
 
-    def lens(gi, carry):
-        @pl.when(gi < g)
-        def _():
-            def short_wait(cb, carry):
-                at = pl.ds(pl.multiple_of(cb * block, block), block)
-                pltpu.make_async_remote_copy(
-                    src_ref=shorts.at[gi, :, :, at],
-                    dst_ref=shorts.at[gi, :, :, at],
-                    send_sem=short_send.at[gi, cb],
-                    recv_sem=short_recv.at[gi, cb],
-                    device_id={"plane": gi},
-                ).wait_recv()
-                return carry
-
-            lax.fori_loop(0, blocks, short_wait, 0)
-            pltpu.make_async_remote_copy(
-                src_ref=longs.at[gi],
-                dst_ref=longs.at[gi],
-                send_sem=long_send.at[gi],
-                recv_sem=long_recv.at[gi],
-                device_id={"plane": gi},
-            ).wait_recv()
-
+    def hessian(gi, field):
         hi, lo = split(longs[gi])
         pieces = coarse_cols // 128
         stacked = [x[:, 128 * b : 128 * b + 128] for x in (hi, lo) for b in range(pieces)]
@@ -383,6 +372,22 @@
         long_wide = jnp.concatenate(upper, axis=1)
         edges = shorts[gi, planes]
         for p in range(planes):
+            center = shorts[gi, p] + jnp.where(
+                row_at < 4, long_wide[4 * p + 1 : 4 * p + 2], long_wide[4 * p + 2 : 4 * p + 3]
+            )
+            top = (edges[2 * p : 2 * p + 1] + long_wide[4 * p : 4 * p + 1]) * low_gain
+            bottom = (
+                edges[2 * p + 1 : 2 * p + 2] + long_wide[4 * p + 3 : 4 * p + 4]
+            ) * high_gain
+            up = jnp.where(row_at == 0, top, pltpu.roll(center, 1, 0))
+            down = jnp.where(row_at == rows - 1, bottom, pltpu.roll(center, rows - 1, 0))
+            field[0, p] = (down - 2.0 * center + up)
+            field[1, p] = (next_col(center) - 2.0 * center + last_col(center))
+            slope = down - up
+            field[2, p] = (next_col(slope) - last_col(slope)) * 0.25
+
+    def advance(gi, field):
+        for p in range(planes):
             k = gi * planes + p
 
             def distance(index):
@@ -400,21 +405,9 @@
             bending = lens_gain * (after - here) / after
             mixing = jnp.concatenate([mixing] * wide, axis=1)
             bending = jnp.concatenate([bending] * wide, axis=1)
-            center = shorts[gi, p] + jnp.where(
-                row_at < 4, long_wide[4 * p + 1 : 4 * p + 2], long_wide[4 * p + 2 : 4 * p + 3]
-            )
-            top = (edges[2 * p : 2 * p + 1] + long_wide[4 * p : 4 * p + 1]) * low_gain
-            bottom = (
-                edges[2 * p + 1 : 2 * p + 2] + long_wide[4 * p + 3 : 4 * p + 4]
-            ) * high_gain
-            up = jnp.where(row_at == 0, top, pltpu.roll(center, 1, 0))
-            down = jnp.where(row_at == rows - 1, bottom, pltpu.roll(center, rows - 1, 0))
-            u11 = (down - 2.0 * center + up) * bending
-            u22 = (next_col(center) - 2.0 * center + last_col(center)) * bending
-            slope = down - up
-            u12 = (next_col(slope) - last_col(slope)) * (0.25 * bending)
             old = [out[e, (p - 2) % planes] for e in range(4)]
             new = [out[e, (p - 1) % planes] for e in range(4)]
+            u11, u22, u12 = [field[i, p] * bending for i in range(3)]
             bent = [
                 u11 * new[0] + u12 * new[2],
                 u11 * new[1] + u12 * new[3],
@@ -423,9 +416,35 @@
             ]
             for e in range(4):
                 out[e, p] = (1.0 - mixing) * old[e] + mixing * new[e] - bent[e]
-        return carry
-
-    lax.fori_loop(0, g + 1, lens, 0)
+
+    def lens(gi, carry):
+        def short_wait(cb, carry):
+            at = pl.ds(pl.multiple_of(cb * block, block), block)
+            pltpu.make_async_remote_copy(
+                src_ref=shorts.at[gi, :, :, at],
+                dst_ref=shorts.at[gi, :, :, at],
+                send_sem=short_send.at[gi, cb],
+                recv_sem=short_recv.at[gi, cb],
+                device_id={"plane": gi},
+            ).wait_recv()
+            return carry
+
+        lax.fori_loop(0, blocks, short_wait, 0)
+        pltpu.make_async_remote_copy(
+            src_ref=longs.at[gi],
+            dst_ref=longs.at[gi],
+            send_sem=long_send.at[gi],
+            recv_sem=long_recv.at[gi],
+            device_id={"plane": gi},
+        ).wait_recv()
+
+        hessian(gi, field_now)
+        advance(gi, field_now)
+        return carry
+
+    hessian(g, field_own)
+    lax.fori_loop(0, g, lens, 0)
+    advance(g, field_own)
 
     def block_sent(cb, carry):
         edge_sent(mass_copy, cb)
@@ -479,10 +498,13 @@
                 pltpu.VMEM((16, 240), bf16),
                 pltpu.VMEM((coarse_cols, coarse_cols), bf16),
                 pltpu.VMEM((coarse_cols, coarse_cols), bf16),
-                pltpu.VMEM((128, block), bf16),
+                pltpu.VMEM((128, span), bf16),
                 pltpu.VMEM((tiles, 8, coarse_cols), f32),
                 pltpu.VMEM((groups, planes + 1, rows, cols), f32),
                 pltpu.VMEM((groups, 16, coarse_cols), f32),
+                pltpu.VMEM((8, cols), f32),
+                pltpu.VMEM((3, planes, rows, cols), f32),
+                pltpu.VMEM((3, planes, rows, cols), f32),
                 dma((2, blocks)),
                 dma((2, blocks)),
                 dma((2, blocks)),

time: 30.4 us -> 32.5 us (1.069)
  Pallas kernels: 27.5 us -> 29.6 us
    pallas_call x1, Pallas kernels: 27.5 us -> 29.6 us  [body(): pl.pallas_call(functools.partial(kernel, tiles, groups), out_shape=jax.Sh...]
where the time goes in v5:
time: 32.5 us; the launch traced here: 32.3 us
  Pallas kernels  29.6 us (91%)
  local copies, waits for them, and re-layouts  2.64 us (8%)
    pallas_call x1, Pallas kernels, body(): pl.pallas_call(functools.partial(kernel, tiles, groups), out_shape=jax.Sh...  29.6 us
    unnamed x12, local copies, waits for them, and re-layouts  2.64 us

profile of v5, /device:TPU:15, one launch (start us, length us, event | category | flops | bytes accessed | tf_op | source)
XLA Modules:
  0.0 32.3 jit_solution(15739226438898062017)
XLA Ops:
  0.0 0.0 copy-start.1
  0.0 0.0 copy-start.4
  0.0 0.0 copy-start.3
  0.0 0.0 copy-start.2
  0.0 0.8 %copy.7.weight = f32[32,9]{1,0:T(8,128)S(1)} copy(f32[32,9]{0,1:T(8,128)} %param.8) | data formatting | bytes 2304 | tf_op args[2]
  0.8 0.0 copy-done.1
  0.8 0.0 copy-done.4
  0.8 0.0 copy-done.3
  0.9 0.0 copy-done.2
  0.9 0.0 copy-start
  0.9 0.9 %copy-done = f32[3,8,2048]{2,1,0:T(8,128)S(1)} copy-done((f32[3,8,2048]{2,1,0:T(8,128)S(1)}, f32[3,8,2048]{2,1,0:T(8,128)}, u32[]{:S(2)}) %copy-start) | copy-done | bytes 196632
  1.8 29.6 %shard_map.64 = f32[4,3,8,2048]{3,2,1,0:T(8,128)S(1)} custom-call(f32[3,8,2048]{2,1,0:T(8,128)S(1)} %copy-done, s32[12]{0:T(128)S(1)} %copy-done.2, f32[32,9]{1,0:T(8,128)S(1)} %copy.7.weight, f32[32]{0:T(128)S(1)} %copy-done.3, f32[32]{0:T(128)S(1)} %copy-done.4, f32[5,5]{1,0:T(8,128)S(1)} %copy-done.1), custom_call_target="tpu_custom_call" | custom-call | tf_op jit(solution)/shard_map/pallas_call | solution.py:487
  31.4 0.9 %copy.9 = f32[4,3,8,2048]{3,2,1,0:T(8,128)} copy(f32[4,3,8,2048]{3,2,1,0:T(8,128)S(1)} %shard_map.64) | data formatting | bytes 1572864
Async XLA Ops:
  0.0 0.8 %copy-start.1 = (f32[5,5]{1,0:T(8,128)S(1)}, f32[5,5]{1,0:T(8,128)}, u32[]{:S(2)}) copy-start(f32[5,5]{1,0:T(8,128)} %short.1) | copy-start | bytes 304
  0.0 0.8 %copy-start.4 = (f32[32]{0:T(128)S(1)}, f32[32]{0:T(128)}, u32[]{:S(2)}) copy-start(f32[32]{0:T(128)} %mix.1) | copy-start | bytes 388
  0.0 0.8 %copy-start.3 = (f32[32]{0:T(128)S(1)}, f32[32]{0:T(128)}, u32[]{:S(2)}) copy-start(f32[32]{0:T(128)} %bias.1) | copy-start | bytes 388
  0.0 0.8 %copy-start.2 = (s32[12]{0:T(128)S(1)}, s32[12]{0:T(128)}, u32[]{:S(2)}) copy-start(s32[12]{0:T(128)} %slot.1) | copy-start | bytes 148
  0.9 0.9 %copy-start = (f32[3,8,2048]{2,1,0:T(8,128)S(1)}, f32[3,8,2048]{2,1,0:T(8,128)}, u32[]{:S(2)}) copy-start(f32[3,8,2048]{2,1,0:T(8,128)} %density.1) | copy-start | bytes 589828

commit v6 on v5

--- a/solution.py
+++ b/solution.py
@@ -10,7 +10,7 @@
 
 lens_gain = 0.25
 pad = 128
-block = 256
+block = 512
 span = 512
 f32 = jnp.float32
 bf16 = jnp.bfloat16
@@ -47,14 +47,17 @@
     has_low = t > 0
     has_high = t < tiles - 1
 
+    def place_of(start, size):
+        return pl.ds(start if isinstance(start, int) else pl.multiple_of(start, pad), size)
+
     def at_block(cb):
-        return pl.ds(pl.multiple_of(cb * block, block), block)
+        return place_of(cb * block, block)
 
     def at_padded(cb):
-        return pl.ds(pl.multiple_of(cb * block + pad, pad), block)
+        return place_of(cb * block + pad, block)
 
     def at_window(cb):
-        return pl.ds(pl.multiple_of(cb * block, block), block + 2 * pad)
+        return place_of(cb * block, block + 2 * pad)
 
     def shifted(x, by):
         moved = x if by == 0 else pltpu.roll(x, (-by) % (block + 2 * pad), 1)
@@ -192,7 +195,8 @@
 
     lax.fori_loop(0, coarse_cols // 64, col_rows, 0)
     mass_own[:, :, pad : pad + cols] = density[...]
-    edge_wait(mass_copy, 0)
+    for cb in range(blocks):
+        edge_wait(mass_copy, cb)
 
     def paint(cb):
         sums = []
@@ -273,43 +277,19 @@
         coarse_copy(j).start()
         return carry
 
-    def paint_step(cb, carry):
-        @pl.when(cb + 1 < blocks)
-        def _():
-            edge_wait(mass_copy, cb + 1)
-
+    for cb in range(blocks):
         paint(cb)
-
-        @pl.when(cb + 1 < blocks)
-        def _():
+        if cb + 1 < blocks:
             edge_start(conv_copy, cb)
 
-        @pl.when(cb == 2)
-        def _():
-            edge_wait(conv_copy, 0)
-
-        @pl.when(cb > 1)
-        def _():
-            edge_wait(conv_copy, cb - 1)
-            short_block(cb - 2)
-
-        return carry
-
-    lax.fori_loop(0, blocks, paint_step, 0)
     pool_columns()
     lax.fori_loop(1, tiles, coarse_start, 0)
     edge_start(conv_copy, blocks - 1)
-    short_rest = max(blocks - 2, 0)
-
-    def short_step(cb, carry):
-        @pl.when(cb + 1 < blocks)
-        def _():
+    edge_wait(conv_copy, 0)
+    for cb in range(blocks):
+        if cb + 1 < blocks:
             edge_wait(conv_copy, cb + 1)
-
         short_block(cb)
-        return carry
-
-    lax.fori_loop(short_rest, blocks, short_step, 0)
 
     def coarse_wait(j, carry):
         source = lax.rem(t + j, tiles)

time: 32.5 us -> 30.9 us (0.951)
  Pallas kernels: 29.6 us -> 28 us
    pallas_call x1, Pallas kernels: 29.6 us -> 28 us  [body(): pl.pallas_call(functools.partial(kernel, tiles, groups), out_shape=jax.Sh...]
where the time goes in v6:
time: 30.9 us; the launch traced here: 30.6 us
  Pallas kernels  28 us (91%)
  local copies, waits for them, and re-layouts  2.64 us (9%)
    pallas_call x1, Pallas kernels, body(): pl.pallas_call(functools.partial(kernel, tiles, groups), out_shape=jax.Sh...  28 us
    unnamed x12, local copies, waits for them, and re-layouts  2.64 us

profile of v6, /device:TPU:15, one launch (start us, length us, event | category | flops | bytes accessed | tf_op | source)
XLA Modules:
  0.0 30.6 jit_solution(8259591600535801113)
XLA Ops:
  0.0 0.0 copy-start.1
  0.0 0.0 copy-start.4
  0.0 0.0 copy-start.3
  0.0 0.0 copy-start.2
  0.0 0.8 %copy.7.weight = f32[32,9]{1,0:T(8,128)S(1)} copy(f32[32,9]{0,1:T(8,128)} %param.8) | data formatting | bytes 2304 | tf_op args[2]
  0.8 0.0 copy-done.1
  0.8 0.0 copy-done.4
  0.8 0.0 copy-done.3
  0.9 0.0 copy-done.2
  0.9 0.0 copy-start
  0.9 0.9 %copy-done = f32[3,8,2048]{2,1,0:T(8,128)S(1)} copy-done((f32[3,8,2048]{2,1,0:T(8,128)S(1)}, f32[3,8,2048]{2,1,0:T(8,128)}, u32[]{:S(2)}) %copy-start) | copy-done | bytes 196632
  1.8 28.0 %shard_map.64 = f32[4,3,8,2048]{3,2,1,0:T(8,128)S(1)} custom-call(f32[3,8,2048]{2,1,0:T(8,128)S(1)} %copy-done, s32[12]{0:T(128)S(1)} %copy-done.2, f32[32,9]{1,0:T(8,128)S(1)} %copy.7.weight, f32[32]{0:T(128)S(1)} %copy-done.3, f32[32]{0:T(128)S(1)} %copy-done.4, f32[5,5]{1,0:T(8,128)S(1)} %copy-done.1), custom_call_target="tpu_custom_call" | custom-call | tf_op jit(solution)/shard_map/pallas_call | solution.py:467
  29.8 0.9 %copy.9 = f32[4,3,8,2048]{3,2,1,0:T(8,128)} copy(f32[4,3,8,2048]{3,2,1,0:T(8,128)S(1)} %shard_map.64) | data formatting | bytes 1572864
Async XLA Ops:
  0.0 0.8 %copy-start.1 = (f32[5,5]{1,0:T(8,128)S(1)}, f32[5,5]{1,0:T(8,128)}, u32[]{:S(2)}) copy-start(f32[5,5]{1,0:T(8,128)} %short.1) | copy-start | bytes 304
  0.0 0.8 %copy-start.4 = (f32[32]{0:T(128)S(1)}, f32[32]{0:T(128)}, u32[]{:S(2)}) copy-start(f32[32]{0:T(128)} %mix.1) | copy-start | bytes 388
  0.0 0.8 %copy-start.3 = (f32[32]{0:T(128)S(1)}, f32[32]{0:T(128)}, u32[]{:S(2)}) copy-start(f32[32]{0:T(128)} %bias.1) | copy-start | bytes 388
  0.0 0.8 %copy-start.2 = (s32[12]{0:T(128)S(1)}, s32[12]{0:T(128)}, u32[]{:S(2)}) copy-start(s32[12]{0:T(128)} %slot.1) | copy-start | bytes 148
  0.9 0.9 %copy-start = (f32[3,8,2048]{2,1,0:T(8,128)S(1)}, f32[3,8,2048]{2,1,0:T(8,128)}, u32[]{:S(2)}) copy-start(f32[3,8,2048]{2,1,0:T(8,128)} %density.1) | copy-start | bytes 589828

commit v7 on v6

--- a/solution.py
+++ b/solution.py
@@ -34,7 +34,7 @@
     mass_own, mass_edge, conv_own, conv_edge, paint_lhs, short_lhs, col_hi, col_lo, spread,
     gathered, shorts, longs, row_sums, field_own, field_now,
     mass_send, mass_recv, conv_send, conv_recv, coarse_send, coarse_recv,
-    short_send, short_recv, long_send, long_recv,
+    short_send, short_recv, long_send, long_recv, pass_send, pass_recv,
 ):
     planes, rows, cols = density.shape
     channels = weight.shape[0]
@@ -230,8 +230,8 @@
 
     def short_copy(cb, to):
         return pltpu.make_async_remote_copy(
-            src_ref=shorts.at[g, :, :, at_block(cb)],
-            dst_ref=shorts.at[g, :, :, at_block(cb)],
+            src_ref=shorts.at[g, 0:planes, :, at_block(cb)],
+            dst_ref=shorts.at[g, 0:planes, :, at_block(cb)],
             send_sem=short_send.at[to, cb],
             recv_sem=short_recv.at[g, cb],
             device_id={"plane": to},
@@ -328,8 +328,6 @@
             out[entry, p] = jnp.full((rows, cols), 1.0 if entry in (0, 3) else 0.0, f32)
     row_at = iota((rows, cols), 0)
     col_at = iota((rows, cols), 1)
-    low_gain = jnp.where(t > 0, 1.0, 0.0)
-    high_gain = jnp.where(t < tiles - 1, 1.0, 0.0)
     slot_total = 2.0 * slots
     wide = cols // 128
 
@@ -355,10 +353,10 @@
             center = shorts[gi, p] + jnp.where(
                 row_at < 4, long_wide[4 * p + 1 : 4 * p + 2], long_wide[4 * p + 2 : 4 * p + 3]
             )
-            top = (edges[2 * p : 2 * p + 1] + long_wide[4 * p : 4 * p + 1]) * low_gain
-            bottom = (
-                edges[2 * p + 1 : 2 * p + 2] + long_wide[4 * p + 3 : 4 * p + 4]
-            ) * high_gain
+            top = edges[2 * p : 2 * p + 1] + long_wide[4 * p : 4 * p + 1]
+            top = jnp.where(has_low, top, 0.0)
+            bottom = edges[2 * p + 1 : 2 * p + 2] + long_wide[4 * p + 3 : 4 * p + 4]
+            bottom = jnp.where(has_high, bottom, 0.0)
             up = jnp.where(row_at == 0, top, pltpu.roll(center, 1, 0))
             down = jnp.where(row_at == rows - 1, bottom, pltpu.roll(center, rows - 1, 0))
             field[0, p] = (down - 2.0 * center + up)
@@ -397,12 +395,26 @@
             for e in range(4):
                 out[e, p] = (1.0 - mixing) * old[e] + mixing * new[e] - bent[e]
 
+    def pass_copy(side, gi, p):
+        row = rows - 1 if side == 0 else 0
+        return pltpu.make_async_remote_copy(
+            src_ref=shorts.at[gi, p, row : row + 1, :],
+            dst_ref=shorts.at[gi, planes, 2 * p + side : 2 * p + side + 1, :],
+            send_sem=pass_send.at[side, gi, p],
+            recv_sem=pass_recv.at[side, gi, p],
+            device_id={"tile": lax.rem(t + (1 if side == 0 else tiles - 1), tiles)},
+        )
+
+    def pass_all(gi, todo):
+        for p in range(planes):
+            todo(lambda side, cb: pass_copy(side, cb, p), gi)
+
     def lens(gi, carry):
         def short_wait(cb, carry):
             at = pl.ds(pl.multiple_of(cb * block, block), block)
             pltpu.make_async_remote_copy(
-                src_ref=shorts.at[gi, :, :, at],
-                dst_ref=shorts.at[gi, :, :, at],
+                src_ref=shorts.at[gi, 0:planes, :, at],
+                dst_ref=shorts.at[gi, 0:planes, :, at],
                 send_sem=short_send.at[gi, cb],
                 recv_sem=short_recv.at[gi, cb],
                 device_id={"plane": gi},
@@ -410,6 +422,7 @@
             return carry
 
         lax.fori_loop(0, blocks, short_wait, 0)
+        pass_all(gi, edge_start)
         pltpu.make_async_remote_copy(
             src_ref=longs.at[gi],
             dst_ref=longs.at[gi],
@@ -418,6 +431,7 @@
             device_id={"plane": gi},
         ).wait_recv()
 
+        pass_all(gi, edge_wait)
         hessian(gi, field_now)
         advance(gi, field_now)
         return carry
@@ -432,6 +446,12 @@
         return carry
 
     lax.fori_loop(0, blocks, block_sent, 0)
+
+    def passed(gi, carry):
+        pass_all(gi, edge_sent)
+        return carry
+
+    lax.fori_loop(0, g, passed, 0)
 
     def coarse_sent(j, carry):
         coarse_copy(j).wait_send()
@@ -495,6 +515,8 @@
                 dma((groups, blocks)),
                 dma((groups,)),
                 dma((groups,)),
+                dma((2, groups, planes)),
+                dma((2, groups, planes)),
             ],
             compiler_params=pltpu.CompilerParams(
                 collective_id=0, has_side_effects=True, vmem_limit_bytes=48 * 1024 * 1024

time: 30.9 us -> 35.5 us (1.15)
  Pallas kernels: 28 us -> 32.2 us
    pallas_call x1, Pallas kernels: 28 us -> 32.2 us  [body(): pl.pallas_call(functools.partial(kernel, tiles, groups), out_shape=jax.Sh...]
where the time goes in v7:
time: 35.5 us; the launch traced here: 34.9 us
  Pallas kernels  32.2 us (91%)
  local copies, waits for them, and re-layouts  2.64 us (7%)
    pallas_call x1, Pallas kernels, body(): pl.pallas_call(functools.partial(kernel, tiles, groups), out_shape=jax.Sh...  32.2 us
    unnamed x12, local copies, waits for them, and re-layouts  2.64 us

profile of v7, /device:TPU:15, one launch (start us, length us, event | category | flops | bytes accessed | tf_op | source)
XLA Modules:
  0.0 34.9 jit_solution(3541459051524000731)
XLA Ops:
  0.0 0.0 copy-start.1
  0.0 0.0 copy-start.4
  0.0 0.0 copy-start.3
  0.0 0.0 copy-start.2
  0.0 0.8 %copy.7.weight = f32[32,9]{1,0:T(8,128)S(1)} copy(f32[32,9]{0,1:T(8,128)} %param.8) | data formatting | bytes 2304 | tf_op args[2]
  0.8 0.0 copy-done.1
  0.8 0.0 copy-done.4
  0.8 0.0 copy-done.3
  0.9 0.0 copy-done.2
  0.9 0.0 copy-start
  0.9 0.9 %copy-done = f32[3,8,2048]{2,1,0:T(8,128)S(1)} copy-done((f32[3,8,2048]{2,1,0:T(8,128)S(1)}, f32[3,8,2048]{2,1,0:T(8,128)}, u32[]{:S(2)}) %copy-start) | copy-done | bytes 196632
  1.8 32.2 %shard_map.64 = f32[4,3,8,2048]{3,2,1,0:T(8,128)S(1)} custom-call(f32[3,8,2048]{2,1,0:T(8,128)S(1)} %copy-done, s32[12]{0:T(128)S(1)} %copy-done.2, f32[32,9]{1,0:T(8,128)S(1)} %copy.7.weight, f32[32]{0:T(128)S(1)} %copy-done.3, f32[32]{0:T(128)S(1)} %copy-done.4, f32[5,5]{1,0:T(8,128)S(1)} %copy-done.1), custom_call_target="tpu_custom_call" | custom-call | tf_op jit(solution)/shard_map/pallas_call | solution.py:487
  34.0 0.9 %copy.9 = f32[4,3,8,2048]{3,2,1,0:T(8,128)} copy(f32[4,3,8,2048]{3,2,1,0:T(8,128)S(1)} %shard_map.64) | data formatting | bytes 1572864
Async XLA Ops:
  0.0 0.8 %copy-start.1 = (f32[5,5]{1,0:T(8,128)S(1)}, f32[5,5]{1,0:T(8,128)}, u32[]{:S(2)}) copy-start(f32[5,5]{1,0:T(8,128)} %short.1) | copy-start | bytes 304
  0.0 0.8 %copy-start.4 = (f32[32]{0:T(128)S(1)}, f32[32]{0:T(128)}, u32[]{:S(2)}) copy-start(f32[32]{0:T(128)} %mix.1) | copy-start | bytes 388
  0.0 0.8 %copy-start.3 = (f32[32]{0:T(128)S(1)}, f32[32]{0:T(128)}, u32[]{:S(2)}) copy-start(f32[32]{0:T(128)} %bias.1) | copy-start | bytes 388
  0.0 0.8 %copy-start.2 = (s32[12]{0:T(128)S(1)}, s32[12]{0:T(128)}, u32[]{:S(2)}) copy-start(s32[12]{0:T(128)} %slot.1) | copy-start | bytes 148
  0.9 0.9 %copy-start = (f32[3,8,2048]{2,1,0:T(8,128)S(1)}, f32[3,8,2048]{2,1,0:T(8,128)}, u32[]{:S(2)}) copy-start(f32[3,8,2048]{2,1,0:T(8,128)} %density.1) | copy-start | bytes 589828

commit v8 on v6

--- a/solution.py
+++ b/solution.py
@@ -34,7 +34,7 @@
     mass_own, mass_edge, conv_own, conv_edge, paint_lhs, short_lhs, col_hi, col_lo, spread,
     gathered, shorts, longs, row_sums, field_own, field_now,
     mass_send, mass_recv, conv_send, conv_recv, coarse_send, coarse_recv,
-    short_send, short_recv, long_send, long_recv,
+    short_send, short_recv, long_send, long_recv, rim_send, rim_recv,
 ):
     planes, rows, cols = density.shape
     channels = weight.shape[0]
@@ -230,10 +230,20 @@
 
     def short_copy(cb, to):
         return pltpu.make_async_remote_copy(
-            src_ref=shorts.at[g, :, :, at_block(cb)],
-            dst_ref=shorts.at[g, :, :, at_block(cb)],
+            src_ref=shorts.at[g, 0:planes, :, at_block(cb)],
+            dst_ref=shorts.at[g, 0:planes, :, at_block(cb)],
             send_sem=short_send.at[to, cb],
             recv_sem=short_recv.at[g, cb],
+            device_id={"plane": to},
+        )
+
+    def rim_copy(source, to):
+        rim = shorts.at[source, planes, 0 : 2 * planes, :]
+        return pltpu.make_async_remote_copy(
+            src_ref=rim,
+            dst_ref=rim,
+            send_sem=rim_send.at[to],
+            recv_sem=rim_recv.at[source],
             device_id={"plane": to},
         )
 
@@ -281,15 +291,24 @@
         paint(cb)
         if cb + 1 < blocks:
             edge_start(conv_copy, cb)
+        if cb == 2:
+            edge_wait(conv_copy, 0)
+        if cb >= 2:
+            edge_wait(conv_copy, cb - 1)
+            short_block(cb - 2)
 
     pool_columns()
     lax.fori_loop(1, tiles, coarse_start, 0)
     edge_start(conv_copy, blocks - 1)
-    edge_wait(conv_copy, 0)
-    for cb in range(blocks):
-        if cb + 1 < blocks:
-            edge_wait(conv_copy, cb + 1)
-        short_block(cb)
+    edge_wait(conv_copy, blocks - 1)
+    short_block(blocks - 2)
+    short_block(blocks - 1)
+
+    def rim_start(to, carry):
+        rim_copy(g, to).start()
+        return carry
+
+    lax.fori_loop(g + 1, groups, rim_start, 0)
 
     def coarse_wait(j, carry):
         source = lax.rem(t + j, tiles)
@@ -401,8 +420,8 @@
         def short_wait(cb, carry):
             at = pl.ds(pl.multiple_of(cb * block, block), block)
             pltpu.make_async_remote_copy(
-                src_ref=shorts.at[gi, :, :, at],
-                dst_ref=shorts.at[gi, :, :, at],
+                src_ref=shorts.at[gi, 0:planes, :, at],
+                dst_ref=shorts.at[gi, 0:planes, :, at],
                 send_sem=short_send.at[gi, cb],
                 recv_sem=short_recv.at[gi, cb],
                 device_id={"plane": gi},
@@ -418,6 +437,7 @@
             device_id={"plane": gi},
         ).wait_recv()
 
+        rim_copy(gi, gi).wait_recv()
         hessian(gi, field_now)
         advance(gi, field_now)
         return carry
@@ -446,6 +466,7 @@
 
         lax.fori_loop(0, blocks, short_sent, 0)
         long_copy(to).wait_send()
+        rim_copy(g, to).wait_send()
         return carry
 
     lax.fori_loop(g + 1, groups, later_sent, 0)
@@ -495,6 +516,8 @@
                 dma((groups, blocks)),
                 dma((groups,)),
                 dma((groups,)),
+                dma((groups,)),
+                dma((groups,)),
             ],
             compiler_params=pltpu.CompilerParams(
                 collective_id=0, has_side_effects=True, vmem_limit_bytes=48 * 1024 * 1024

time: 30.9 us -> 31.1 us (level)
  the two profiles are of different devices: /device:TPU:15 before, /device:TPU:22 now
where the time goes in v8:
time: 31.1 us; the launch traced here: 30.9 us
  Pallas kernels  28.2 us (91%)
  local copies, waits for them, and re-layouts  2.64 us (8%)
    pallas_call x1, Pallas kernels, body(): pl.pallas_call(functools.partial(kernel, tiles, groups), out_shape=jax.Sh...  28.2 us
    unnamed x12, local copies, waits for them, and re-layouts  2.64 us

profile of v8, /device:TPU:22, one launch (start us, length us, event | category | flops | bytes accessed | tf_op | source)
XLA Modules:
  0.0 30.9 jit_solution(3956207408500017569)
XLA Ops:
  0.0 0.0 copy-start.1
  0.0 0.0 copy-start.4
  0.0 0.0 copy-start.3
  0.0 0.0 copy-start.2
  0.0 0.8 %copy.7.weight = f32[32,9]{1,0:T(8,128)S(1)} copy(f32[32,9]{0,1:T(8,128)} %param.8) | data formatting | bytes 2304 | tf_op args[2]
  0.8 0.0 copy-done.1
  0.8 0.0 copy-done.4
  0.8 0.0 copy-done.3
  0.9 0.0 copy-done.2
  0.9 0.0 copy-start
  0.9 0.9 %copy-done = f32[3,8,2048]{2,1,0:T(8,128)S(1)} copy-done((f32[3,8,2048]{2,1,0:T(8,128)S(1)}, f32[3,8,2048]{2,1,0:T(8,128)}, u32[]{:S(2)}) %copy-start) | copy-done | bytes 196632
  1.8 28.2 %shard_map.64 = f32[4,3,8,2048]{3,2,1,0:T(8,128)S(1)} custom-call(f32[3,8,2048]{2,1,0:T(8,128)S(1)} %copy-done, s32[12]{0:T(128)S(1)} %copy-done.2, f32[32,9]{1,0:T(8,128)S(1)} %copy.7.weight, f32[32]{0:T(128)S(1)} %copy-done.3, f32[32]{0:T(128)S(1)} %copy-done.4, f32[5,5]{1,0:T(8,128)S(1)} %copy-done.1), custom_call_target="tpu_custom_call" | custom-call | tf_op jit(solution)/shard_map/pallas_call | solution.py:488
  30.0 0.9 %copy.9 = f32[4,3,8,2048]{3,2,1,0:T(8,128)} copy(f32[4,3,8,2048]{3,2,1,0:T(8,128)S(1)} %shard_map.64) | data formatting | bytes 1572864
Async XLA Ops:
  0.0 0.8 %copy-start.1 = (f32[5,5]{1,0:T(8,128)S(1)}, f32[5,5]{1,0:T(8,128)}, u32[]{:S(2)}) copy-start(f32[5,5]{1,0:T(8,128)} %short.1) | copy-start | bytes 304
  0.0 0.8 %copy-start.4 = (f32[32]{0:T(128)S(1)}, f32[32]{0:T(128)}, u32[]{:S(2)}) copy-start(f32[32]{0:T(128)} %mix.1) | copy-start | bytes 388
  0.0 0.8 %copy-start.3 = (f32[32]{0:T(128)S(1)}, f32[32]{0:T(128)}, u32[]{:S(2)}) copy-start(f32[32]{0:T(128)} %bias.1) | copy-start | bytes 388
  0.0 0.8 %copy-start.2 = (s32[12]{0:T(128)S(1)}, s32[12]{0:T(128)}, u32[]{:S(2)}) copy-start(s32[12]{0:T(128)} %slot.1) | copy-start | bytes 148
  0.9 0.9 %copy-start = (f32[3,8,2048]{2,1,0:T(8,128)S(1)}, f32[3,8,2048]{2,1,0:T(8,128)}, u32[]{:S(2)}) copy-start(f32[3,8,2048]{2,1,0:T(8,128)} %density.1) | copy-start | bytes 589828

commit v9 on v5

--- a/solution.py
+++ b/solution.py
@@ -10,7 +10,7 @@
 
 lens_gain = 0.25
 pad = 128
-block = 256
+block = 512
 span = 512
 f32 = jnp.float32
 bf16 = jnp.bfloat16

time: 32.5 us -> 30.4 us (0.935)
  Pallas kernels: 29.6 us -> 27.5 us
    pallas_call x1, Pallas kernels: 29.6 us -> 27.5 us  [body(): pl.pallas_call(functools.partial(kernel, tiles, groups), out_shape=jax.Sh...]
where the time goes in v9:
time: 30.4 us; the launch traced here: 30.2 us
  Pallas kernels  27.5 us (90%)
  local copies, waits for them, and re-layouts  2.64 us (9%)
    pallas_call x1, Pallas kernels, body(): pl.pallas_call(functools.partial(kernel, tiles, groups), out_shape=jax.Sh...  27.5 us
    unnamed x12, local copies, waits for them, and re-layouts  2.64 us

profile of v9, /device:TPU:15, one launch (start us, length us, event | category | flops | bytes accessed | tf_op | source)
XLA Modules:
  0.0 30.2 jit_solution(1417611813013638778)
XLA Ops:
  0.0 0.0 copy-start.1
  0.0 0.0 copy-start.4
  0.0 0.0 copy-start.3
  0.0 0.0 copy-start.2
  0.0 0.8 %copy.7.weight = f32[32,9]{1,0:T(8,128)S(1)} copy(f32[32,9]{0,1:T(8,128)} %param.8) | data formatting | bytes 2304 | tf_op args[2]
  0.8 0.0 copy-done.1
  0.8 0.0 copy-done.4
  0.8 0.0 copy-done.3
  0.9 0.0 copy-done.2
  0.9 0.0 copy-start
  0.9 0.9 %copy-done = f32[3,8,2048]{2,1,0:T(8,128)S(1)} copy-done((f32[3,8,2048]{2,1,0:T(8,128)S(1)}, f32[3,8,2048]{2,1,0:T(8,128)}, u32[]{:S(2)}) %copy-start) | copy-done | bytes 196632
  1.8 27.5 %shard_map.64 = f32[4,3,8,2048]{3,2,1,0:T(8,128)S(1)} custom-call(f32[3,8,2048]{2,1,0:T(8,128)S(1)} %copy-done, s32[12]{0:T(128)S(1)} %copy-done.2, f32[32,9]{1,0:T(8,128)S(1)} %copy.7.weight, f32[32]{0:T(128)S(1)} %copy-done.3, f32[32]{0:T(128)S(1)} %copy-done.4, f32[5,5]{1,0:T(8,128)S(1)} %copy-done.1), custom_call_target="tpu_custom_call" | custom-call | tf_op jit(solution)/shard_map/pallas_call | solution.py:487
  29.3 0.9 %copy.9 = f32[4,3,8,2048]{3,2,1,0:T(8,128)} copy(f32[4,3,8,2048]{3,2,1,0:T(8,128)S(1)} %shard_map.64) | data formatting | bytes 1572864
Async XLA Ops:
  0.0 0.8 %copy-start.1 = (f32[5,5]{1,0:T(8,128)S(1)}, f32[5,5]{1,0:T(8,128)}, u32[]{:S(2)}) copy-start(f32[5,5]{1,0:T(8,128)} %short.1) | copy-start | bytes 304
  0.0 0.8 %copy-start.4 = (f32[32]{0:T(128)S(1)}, f32[32]{0:T(128)}, u32[]{:S(2)}) copy-start(f32[32]{0:T(128)} %mix.1) | copy-start | bytes 388
  0.0 0.8 %copy-start.3 = (f32[32]{0:T(128)S(1)}, f32[32]{0:T(128)}, u32[]{:S(2)}) copy-start(f32[32]{0:T(128)} %bias.1) | copy-start | bytes 388
  0.0 0.8 %copy-start.2 = (s32[12]{0:T(128)S(1)}, s32[12]{0:T(128)}, u32[]{:S(2)}) copy-start(s32[12]{0:T(128)} %slot.1) | copy-start | bytes 148
  0.9 0.9 %copy-start = (f32[3,8,2048]{2,1,0:T(8,128)S(1)}, f32[3,8,2048]{2,1,0:T(8,128)}, u32[]{:S(2)}) copy-start(f32[3,8,2048]{2,1,0:T(8,128)} %density.1) | copy-start | bytes 589828
